TPU v7x, 32 devices: a whole 2x2x4 slice. The times are simulated.
32 devices in a mesh: groups: 2 (over y), wide: 8 (over z, core), narrow: 2 (over x).
Axes of the slice: x: 2, y: 2, z: 4, core: 2. Of those that a mesh axis runs over, the one named last changes fastest.
Arguments:
- tokens: bfloat16 [192, 16384], P(('groups', 'narrow'), 'wide'), parts along dimension 0, may hold values from -64 to 64
- norm_gain: bfloat16 [16384], P('wide'), may hold values from 0.099609375 to 1.8984375
- w_query: bfloat16 [16384, 16384], P('wide', 'narrow'), may hold values from -0.046875 to 0.046875
- w_key: bfloat16 [16384, 1024], P('wide', 'narrow'), may hold values from -0.046875 to 0.046875
- w_value: bfloat16 [16384, 1024], P('wide', 'narrow'), may hold values from -0.046875 to 0.046875
- w_out: bfloat16 [16384, 16384], P('narrow', 'wide'), may hold values from -0.046875 to 0.046875
- cache_key: bfloat16 [192, 256, 1024], P(('groups', 'wide'), None, 'narrow'), parts along dimension 0, may hold values from -400 to 400
- cache_value: bfloat16 [192, 256, 1024], P(('groups', 'wide'), None, 'narrow'), parts along dimension 0, may hold values from -24 to 24
- lengths: int32 [192], P('groups'), parts along dimension 0, may hold values from 2 to 256, as said below
Outputs:
- attended: bfloat16 [192, 16384], P(('groups', 'narrow'), 'wide'), parts along dimension 0
There are 2 independent parts, one for each index of `groups`. A program takes and returns all parts, laid end to end along the dimension named above; an argument that names none is the same for every part. Nothing has to cross between parts.
Inputs may be any that keep to these rules, and one draw needn't show every extreme that they name: `lengths`: each row has at least two filled slots, and some row fills all 256 slots.
All inputs are finite; a program needn't handle non-finite values.
Results may differ from a plain program's by a relative error of at most 0.012.
The roundings to bfloat16 on the way count: a program that leaves them out, or rounds other values in their place, can miss the bound.
Values may be sent and summed in bfloat16 or wider, within the bound.
A program may use at most 192 MiB of HBM per device.

v0:
```python
import jax
import jax.numpy as jnp
from jax import lax
from jax.sharding import PartitionSpec as P

D = 16384
HD = 128


rope_base = 500000.0
norm_eps = 1e-05


def rotate(vectors, positions):
    half_dim = vectors.shape[-1] // 2
    frequency = rope_base ** (-jnp.arange(half_dim, dtype=jnp.float32) / half_dim)
    angles = positions.astype(jnp.float32)[:, None] * frequency[None, :]
    cosine = jnp.cos(angles)[:, None, :]
    sines = jnp.sin(angles)[:, None, :]
    leading_half = vectors[..., :half_dim]
    trailing_half = vectors[..., half_dim:]
    return jnp.concatenate(
        [
            leading_half * cosine - trailing_half * sines,
            trailing_half * cosine + leading_half * sines,
        ],
        axis=-1,
    )


def attend(queries, key_new, value_new, cache_key, cache_value, lengths):
    batch_rows, head_count, head_dim = queries.shape
    group_count = key_new.shape[1]
    per_group = head_count // group_count
    token_count = cache_key.shape[1]
    grouped = queries.reshape(batch_rows, group_count, per_group, head_dim)
    cached_keys = cache_key.reshape(batch_rows, token_count, group_count, head_dim)
    cached_values = cache_value.reshape(batch_rows, token_count, group_count, head_dim)
    score_scale = head_dim ** (-0.5)
    scores = (
        jnp.einsum("rgqd,rtgd->rgqt", grouped, cached_keys, preferred_element_type=jnp.float32)
        * score_scale
    )
    own_score = (
        jnp.einsum("rgqd,rgd->rgq", grouped, key_new, preferred_element_type=jnp.float32)
        * score_scale
    )
    usable = (jnp.arange(token_count)[None, :] < lengths[:, None])[:, None, None, :]
    highest = jnp.maximum(jnp.max(jnp.where(usable, scores, -1e30), axis=-1), own_score)
    weights = jnp.where(usable, jnp.exp(scores - highest[..., None]), 0.0)
    own_weight = jnp.exp(own_score - highest)
    denominator = jnp.sum(weights, axis=-1) + own_weight
    blended = jnp.einsum(
        "rgqt,rtgd->rgqd",
        weights.astype(jnp.bfloat16),
        cached_values,
        preferred_element_type=jnp.float32,
    )
    blended = blended + own_weight[..., None] * value_new.astype(jnp.float32)[:, :, None, :]
    return (
        (blended / denominator[..., None])
        .astype(jnp.bfloat16)
        .reshape(batch_rows, head_count * head_dim)
    )


def per_device(tokens, norm_gain, w_query, w_key, w_value, w_out, cache_key, cache_value, lengths):
    all_rows = lax.all_gather(tokens, "narrow", axis=0, tiled=True)
    features = all_rows.astype(jnp.float32)
    squares = lax.psum_scatter(
        jnp.sum(features * features, axis=1), "wide", scatter_dimension=0, tiled=True
    )
    inverse = lax.rsqrt(squares / D + norm_eps)
    scaled = (features * norm_gain.astype(jnp.float32)[None, :]).astype(jnp.bfloat16)
    own_rows = cache_key.shape[0]
    row_start = lax.axis_index("wide") * own_rows
    query_cols = w_query.shape[1]
    kv_cols = w_key.shape[1]
    whole_sums = lax.psum(
        jnp.concatenate(
            [
                jnp.dot(scaled, w_query, preferred_element_type=jnp.float32),
                jnp.dot(scaled, w_key, preferred_element_type=jnp.float32),
                jnp.dot(scaled, w_value, preferred_element_type=jnp.float32),
            ],
            axis=1,
        ),
        "wide",
    )
    summed = lax.dynamic_slice_in_dim(whole_sums, row_start, own_rows, 0)
    summed = summed * inverse[:, None]
    own_lengths = lax.dynamic_slice_in_dim(lengths, row_start, own_rows, 0)
    queries = rotate(
        summed[:, :query_cols].reshape(own_rows, query_cols // HD, HD), own_lengths
    ).astype(jnp.bfloat16)
    key_new = rotate(
        summed[:, query_cols : query_cols + kv_cols].reshape(own_rows, kv_cols // HD, HD),
        own_lengths,
    ).astype(jnp.bfloat16)
    value_new = (
        summed[:, query_cols + kv_cols :].reshape(own_rows, kv_cols // HD, HD).astype(jnp.bfloat16)
    )
    heads_out = attend(queries, key_new, value_new, cache_key, cache_value, own_lengths)
    partials = jnp.dot(
        lax.all_gather(heads_out, "wide", axis=0, tiled=True),
        w_out,
        preferred_element_type=jnp.float32,
    )
    return lax.psum_scatter(
        partials.astype(jnp.bfloat16), "narrow", scatter_dimension=0, tiled=True
    )


def solution(mesh):
    return jax.shard_map(
        per_device,
        mesh=mesh,
        in_specs=(
            P(("groups", "narrow"), "wide"),
            P("wide"),
            P("wide", "narrow"),
            P("wide", "narrow"),
            P("wide", "narrow"),
            P("narrow", "wide"),
            P(("groups", "wide"), None, "narrow"),
            P(("groups", "wide"), None, "narrow"),
            P("groups"),
        ),
        out_specs=P(("groups", "narrow"), "wide"),
        check_vma=False,
    )
```

profile of v0, /device:TPU:0, one launch (start us, length us, event | category | flops | bytes accessed | tf_op | source)
XLA Modules:
  0.0 195.8 jit_solution(6238462906124928444)
XLA Ops:
  6.5 0.8 convert_element_type.42
  7.4 8.9 %all_gather.6 = bf16[96,2048]{1,0:T(8,128)(2,1)S(1)} all-gather(bf16[48,2048]{1,0:T(8,128)(2,1)} %param.9), channel_id=1, replica_groups=mesh['groups'=2,'wide'=8,'narrow'=2] {'narrow'}, dimensions={0}, use_global_device_ids=true | all-gather | bytes 589824 | tf_op jit(solution)/shard_map/all_gather | solution.py:68
  16.3 2.0 %fusion.28 = f32[96,512]{1,0:T(8,128)S(1)} fusion(bf16[2048,512]{1,0:T(8,128)(2,1)} %param.12, bf16[96,2048]{1,0:T(8,128)(2,1)S(1)} %all_gather.6, f32[2048]{0:T(1024)S(1)} %convert_element_type.42), kind=kOutput, calls=%fused_computation.27 | convolution fusion | flops 201916416 | bytes 2695168 | tf_op jit(solution)/shard_map/dot_general | solution.py:83
  18.3 0.5 fusion.26
  18.8 13.3 %fusion.30 = f32[96,8192]{1,0:T(8,128)S(1)} fusion(bf16[2048,8192]{1,0:T(8,128)(2,1)} %param.11, bf16[96,2048]{1,0:T(8,128)(2,1)S(1)} %all_gather.6, f32[2048]{0:T(1024)S(1)} %convert_element_type.42), kind=kOutput, calls=%fused_computation.28 | convolution fusion | flops 3221815296 | bytes 37101568 | tf_op jit(solution)/shard_map/dot_general | solution.py:82
  32.2 2.1 %pad_maximum_fusion = f32[96,9216]{1,0:T(8,128)} fusion(f32[96,512]{1,0:T(8,128)S(1)} %fusion.26, f32[96,512]{1,0:T(8,128)S(1)} %fusion.28, f32[96,8192]{1,0:T(8,128)S(1)} %fusion.30), kind=kLoop, calls=%fused_computation | loop fusion | flops 1769472 | bytes 7077888 | tf_op jit(solution)/shard_map/concatenate | solution.py:80
  34.3 0.6 copy-done.5
  34.9 0.6 dynamic-slice
  36.1 0.2 fusion.19
  36.3 16.4 %all-reduce = f32[96]{0:T(128)S(1)} all-reduce(f32[96]{0:T(128)S(1)} %fusion.19), channel_id=2, replica_groups=mesh['groups'=2,'wide'=8,'narrow'=2] {'wide'}, use_global_device_ids=true, to_apply=%region_2.0.clone | all-reduce | flops 96 | bytes 768
  53.1 67.2 %all-reduce.3.cloned.1.call-done = f32[96,9216]{1,0:T(8,128)} async-done(((f32[96,9216]{1,0:T(8,128)}), f32[96,9216]{1,0:T(8,128)}) %all-reduce.3.cloned.1.call-update) | async-done | bytes 3538960 | tf_op jit(solution)/shard_map/psum | solution.py:79
  120.3 1.3 dynamic-slice_multiply_fusion
  121.6 0.8 slice.29
  122.4 1.1 copy.20
  123.6 0.2 subtract_convert_fusion
  124.0 0.3 fusion.32
  124.3 1.1 select_reduce_fusion
  125.4 0.4 fusion.20
  125.8 0.6 fusion.15
  126.4 0.9 reshape.109
  127.3 29.2 %all-gather.3.cloned.1.call-done = bf16[8,12,8192]{2,1,0:T(8,128)(2,1)} async-done(((bf16[1,12,8192]{2,1,0:T(8,128)(2,1)}), bf16[8,12,8192]{2,1,0:T(8,128)(2,1)}) %all-gather.3.cloned.1.call-update) | async-done | bytes 1572880 | tf_op jit(solution)/shard_map/all_gather | solution.py:105
  156.6 2.6 %reshape.110 = bf16[96,8192]{1,0:T(8,128)(2,1)} reshape(bf16[8,12,8192]{2,1,0:T(8,128)(2,1)} %all-gather.3.cloned.1.call-done) | data formatting | bytes 3145728
  159.2 17.3 %convolution_convert_fusion = bf16[96,2048]{1,0:T(8,128)(2,1)} fusion(bf16[96,8192]{1,0:T(8,128)(2,1)} %reshape.110, bf16[8192,2048]{1,0:T(8,128)(2,1)} %param.14), kind=kOutput, calls=%fused_computation.7 | convolution fusion | flops 3221422080 | bytes 35520512 | tf_op jit(solution)/shard_map/dot_general | solution.py:104
  176.5 12.8 %reduce-scatter.2.cloned.1.call-done = bf16[48,2048]{1,0:T(8,128)(2,1)} async-done(((bf16[96,2048]{1,0:T(8,128)(2,1)}), bf16[48,2048]{1,0:T(8,128)(2,1)}) %reduce-scatter.2.cloned.1.call-update) | async-done | bytes 196624 | tf_op jit(solution)/shard_map/reduce_scatter | solution.py:109
  (31 shorter events, 0.8 us)
Async XLA Ops:
  6.5 117.7 %copy-start = (bf16[12,256,512]{2,1,0:T(8,128)(2,1)S(1)}, bf16[12,256,512]{2,1,0:T(8,128)(2,1)}, u32[]{:S(2)}) copy-start(bf16[12,256,512]{2,1,0:T(8,128)(2,1)} %param.15) | copy-start | bytes 9437188
  6.5 113.7 %all-reduce.3.cloned.1.call-start = ((), (), s32[]{:S(2)}) async-start(), calls=%async_computation.1 | async-start | bytes 7077888 | tf_op jit(solution)/shard_map/psum | solution.py:79
  6.5 11.8 %copy-start.2 = (bf16[2048,512]{1,0:T(8,128)(2,1)S(1)}, bf16[2048,512]{1,0:T(8,128)(2,1)}, u32[]{:S(2)}) copy-start(bf16[2048,512]{1,0:T(8,128)(2,1)} %param.13) | copy-start | bytes 6291460
  34.2 0.7 copy-start.5
  34.2 18.6 %copy-start.3 = (s32[96]{0:T(128)S(1)}, s32[96]{0:T(128)}, u32[]{:S(2)}) copy-start(s32[96]{0:T(128)} %param.17) | copy-start | bytes 1156
  34.2 122.3 %all-gather.3.cloned.1.call-start = ((), (), s32[]{:S(2)}) async-start(), calls=%async_computation.3 | async-start | bytes 2359296 | tf_op jit(solution)/shard_map/all_gather | solution.py:105
  123.8 2.0 %copy-start.4 = (bf16[12,256,512]{2,1,0:T(8,128)(2,1)S(1)}, bf16[12,256,512]{2,1,0:T(8,128)(2,1)}, u32[]{:S(2)}) copy-start(bf16[12,256,512]{2,1,0:T(8,128)(2,1)} %param.16) | copy-start | bytes 9437188
  127.3 62.0 %reduce-scatter.2.cloned.1.call-start = ((), (), s32[]{:S(2)}) async-start(), calls=%async_computation.2 | async-start | bytes 589824 | tf_op jit(solution)/shard_map/reduce_scatter | solution.py:109
  159.2 30.1 %copy-start.1 = (bf16[12,256,512]{2,1,0:T(8,128)(2,1)S(1)}, bf16[12,256,512]{2,1,0:T(8,128)(2,1)}, u32[]{:S(2)}) copy-start(bf16[12,256,512]{2,1,0:T(8,128)(2,1)} %param.15) | copy-start | bytes 9437188
Sparse Core Ops, SparseCore 0:
  34.4 85.8 all-reduce.2
  127.4 29.1 all-gather.2
  176.7 12.5 reduce-scatter.1
where the time goes:
time: 196 us
  waiting for transfers between devices  109 us (56%)
  matrix products  35.1 us (18%)
  blocking collectives  25.3 us (13%)
  between operations  13.9 us (7%)
  local copies, waits for them, and re-layouts  6.69 us (3%)
  other arithmetic  5.47 us (3%)
    psum x1, waiting for transfers between devices, per_device(): lax.psum(jnp.concatenate([jnp.dot(scaled, w_query, preferred_element_type...  67.2 us
    all_gather x1, waiting for transfers between devices, per_device(): lax.all_gather(heads_out, 'wide', axis=0, tiled=True)  29.2 us
    dot_general x1, matrix products, per_device(): jnp.dot(lax.all_gather(heads_out, 'wide', axis=0, tiled=True), w_out, pre...  17.3 us
    unnamed x1, blocking collectives  16.4 us
    dot_general x1, matrix products, per_device(): jnp.dot(scaled, w_query, preferred_element_type=jnp.float32)  13.3 us
    reduce_scatter x1, waiting for transfers between devices, per_device(): lax.psum_scatter(partials.astype(jnp.bfloat16), 'narrow', scatter_dimensi...  12.8 us
    all_gather x1, blocking collectives, per_device(): all_rows = lax.all_gather(tokens, 'narrow', axis=0, tiled=True)  8.89 us
    unnamed x16, local copies, waits for them, and re-layouts  5.81 us
  transfers between devices with their start and end apart: 3, of which 3 were waited for; matrix products, arithmetic and copies ran while one was open for 1% of the time, Pallas kernels for 0%

commit v1 on v0

--- a/solution.py
+++ b/solution.py
@@ -1,10 +1,18 @@
+import functools
+
 import jax
 import jax.numpy as jnp
 from jax import lax
+from jax.experimental import pallas as pl
+from jax.experimental.pallas import tpu as pltpu
 from jax.sharding import PartitionSpec as P
 
 D = 16384
 HD = 128
+PAD = 16
+PARTS = 4
+TILE = 256
+MESH = pl.DeviceIdType.MESH
 
 
 rope_base = 500000.0
@@ -64,31 +72,397 @@
     )
 
 
-def per_device(tokens, norm_gain, w_query, w_key, w_value, w_out, cache_key, cache_value, lengths):
+def remote(src, dst, send_sem, recv_sem, device):
+    return pltpu.make_async_remote_copy(
+        src_ref=src,
+        dst_ref=dst,
+        send_sem=send_sem,
+        recv_sem=recv_sem,
+        device_id=device,
+        device_id_type=MESH,
+    )
+
+
+def sums_kernel(
+    nz, steps, x_ref, sq_ref, out_ref, sq_out_ref,
+    core_recv, core_sq, send_buf, recv_buf, sq_send, sq_recv,
+    core_ss, core_rs, csq_s, csq_r, z_ss, z_rs, zsq_ss, zsq_rs, fin_ss, fin_rs,
+):
+    me = lax.axis_index("wide")
+    z, core = me // 2, lax.rem(me, 2)
+    sibling = {"wide": me + 1 - 2 * core}
+    rows, cols = x_ref.shape
+    block = rows // nz
+    half = cols // 2
+    width = half // steps
+    peers = [lax.rem(z + d, nz) for d in range(1, nz)]
+    barrier = pltpu.get_barrier_semaphore()
+    pl.semaphore_signal(barrier, inc=1, device_id=sibling, device_id_type=MESH)
+    for peer in peers:
+        pl.semaphore_signal(
+            barrier, inc=1, device_id={"wide": peer * 2 + core}, device_id_type=MESH
+        )
+    pl.semaphore_wait(barrier, nz)
+
+    def columns(which, t):
+        return pl.ds(pl.multiple_of(which * half + t * width, 128), width)
+
+    csq = remote(sq_ref, core_sq, csq_s, csq_r, sibling)
+    csq.start()
+    core_copies = []
+    for t in range(steps):
+        copy = remote(
+            x_ref.at[:, columns(1 - core, t)],
+            core_recv.at[t],
+            core_ss.at[t],
+            core_rs.at[t],
+            sibling,
+        )
+        copy.start()
+        core_copies.append(copy)
+    copies = []
+    csq.wait_recv()
+    for d, peer in enumerate(peers):
+        span = pl.ds(pl.multiple_of(peer * block, 8), block)
+        sq_send[d] = sq_ref[span, :] + core_sq[span, :]
+        copy = remote(
+            sq_send.at[d], sq_recv.at[d], zsq_ss.at[d], zsq_rs.at[d], {"wide": peer * 2 + core}
+        )
+        copy.start()
+        copies.append(copy)
+    z_copies = []
+    for t in range(steps):
+        core_copies[t].wait_recv()
+        row = []
+        for d, peer in enumerate(peers):
+            span = pl.ds(pl.multiple_of(peer * block, 8), block)
+            both = x_ref[span, columns(core, t)] + core_recv[t, span, :]
+            send_buf[t, d] = jnp.concatenate(
+                [both[:, : width // 2], both[:, width // 2 :]], axis=0
+            ).astype(jnp.bfloat16)
+            copy = remote(
+                send_buf.at[t, d],
+                recv_buf.at[t, d],
+                z_ss.at[t, d],
+                z_rs.at[t, d],
+                {"wide": peer * 2 + core},
+            )
+            copy.start()
+            row.append(copy)
+        z_copies.append(row)
+    mine = pl.ds(pl.multiple_of(z * block, 8), block)
+    total = sq_ref[mine, :] + core_sq[mine, :]
+    for d in range(nz - 1):
+        copies[d].wait_recv()
+        total = total + sq_recv[d]
+    sq_out_ref[...] = total
+    finals = []
+    for t in range(steps):
+        acc = x_ref[mine, columns(core, t)] + core_recv[t, mine, :]
+        left, right = acc[:, : width // 2], acc[:, width // 2 :]
+        for d in range(nz - 1):
+            z_copies[t][d].wait_recv()
+            got = recv_buf[t, d].astype(jnp.float32)
+            left = left + got[:block]
+            right = right + got[block:]
+        out_ref[:, columns(core, t)] = jnp.concatenate([left, right], axis=1)
+        copy = remote(
+            out_ref.at[:, columns(core, t)],
+            out_ref.at[:, columns(core, t)],
+            fin_ss.at[t],
+            fin_rs.at[t],
+            sibling,
+        )
+        copy.start()
+        finals.append(copy)
+    csq.wait_send()
+    for copy in core_copies + copies + sum(z_copies, []):
+        copy.wait_send()
+    for t in range(steps):
+        finals[t].wait_send()
+        remote(
+            out_ref.at[:, columns(1 - core, t)],
+            out_ref.at[:, columns(1 - core, t)],
+            fin_ss.at[t],
+            fin_rs.at[t],
+            sibling,
+        ).wait_recv()
+
+
+def sum_over_wide(x, sq, n_wide):
+    nz = n_wide // 2
+    rows, cols = x.shape
+    block = rows // nz
+    steps = 3
+    width = cols // 2 // steps
+    vmem = pl.BlockSpec(memory_space=pltpu.VMEM)
+    dma = pltpu.SemaphoreType.DMA
+    return pl.pallas_call(
+        functools.partial(sums_kernel, nz, steps),
+        out_shape=(
+            jax.ShapeDtypeStruct((block, cols), jnp.float32),
+            jax.ShapeDtypeStruct((block, 128), jnp.float32),
+        ),
+        in_specs=[vmem, vmem],
+        out_specs=(vmem, vmem),
+        scratch_shapes=[
+            pltpu.VMEM((steps, rows, width), jnp.float32),
+            pltpu.VMEM((rows, 128), jnp.float32),
+            pltpu.VMEM((steps, nz - 1, 2 * block, width // 2), jnp.bfloat16),
+            pltpu.VMEM((steps, nz - 1, 2 * block, width // 2), jnp.bfloat16),
+            pltpu.VMEM((nz - 1, block, 128), jnp.float32),
+            pltpu.VMEM((nz - 1, block, 128), jnp.float32),
+            dma((steps,)),
+            dma((steps,)),
+            dma,
+            dma,
+            dma((steps, nz - 1)),
+            dma((steps, nz - 1)),
+            dma((nz - 1,)),
+            dma((nz - 1,)),
+            dma((steps,)),
+            dma((steps,)),
+        ],
+        compiler_params=pltpu.CompilerParams(
+            collective_id=0, has_side_effects=True, vmem_limit_bytes=48 << 20
+        ),
+    )(x, sq)
+
+
+def project_kernel(
+    nz, nn, own_rows, heads_ref, w_ref, out_ref,
+    held, weights, parts, recv_parts,
+    w_sem, right_s, left_s, right_r, left_r, sib_s, sib_r, x_ss, x_rs,
+):
+    me = lax.axis_index("wide")
+    across = lax.axis_index("narrow")
+    z, core = me // 2, lax.rem(me, 2)
+    sib_index = me + 1 - 2 * core
+    sibling = {"wide": sib_index}
+    right, left = {"wide": me + 2}, {"wide": me - 2}
+    has_right, has_left = z < nz - 1, z > 0
+    n_wide = 2 * nz
+    tiles = w_ref.shape[1] // TILE
+    chunk = w_ref.shape[0] // PARTS
+    out_rows = out_ref.shape[0]
+
+    w_copies = []
+    for t in range(tiles):
+        cols = pl.ds(t * TILE, TILE)
+        copy = pltpu.make_async_copy(w_ref.at[:, cols], weights.at[t], w_sem.at[t])
+        copy.start()
+        w_copies.append(copy)
+
+    barrier = pltpu.get_barrier_semaphore()
+
+    def greet(device):
+        pl.semaphore_signal(barrier, inc=1, device_id=device, device_id_type=MESH)
+
+    greet(sibling)
+    for d in range(1, nn):
+        greet({"narrow": lax.rem(across + d, nn)})
+
+    @pl.when(has_right)
+    def _():
+        greet(right)
+
+    @pl.when(has_left)
+    def _():
+        greet(left)
+
+    ends = jnp.where(has_right, 1, 0) + jnp.where(has_left, 1, 0)
+    pl.semaphore_wait(barrier, nn + ends)
+
+    def to_right(h):
+        slot = held.at[me - 2 * h]
+        return remote(slot, slot, right_s.at[h], right_r.at[h], right)
+
+    def to_left(h):
+        slot = held.at[me + 2 * h]
+        return remote(slot, slot, left_s.at[h], left_r.at[h], left)
+
+    def to_sibling(k, index):
+        return remote(held.at[index], held.at[index], sib_s.at[k], sib_r.at[k], sibling)
+
+    held[me] = heads_ref[...]
+
+    @pl.when(has_right)
+    def _():
+        to_right(0).start()
+
+    @pl.when(has_left)
+    def _():
+        to_left(0).start()
+
+    to_sibling(0, me).start()
+    for h in range(1, nz):
+
+        @pl.when(z - h >= 0)
+        def _():
+            slot = held.at[me - 2 * h]
+            remote(slot, slot, right_s.at[h - 1], right_r.at[h - 1], left).wait_recv()
+
+            @pl.when(has_right)
+            def _():
+                to_right(h).start()
+
+            to_sibling(h, me - 2 * h).start()
+
+        @pl.when(z + h < nz)
+        def _():
+            slot = held.at[me + 2 * h]
+            remote(slot, slot, left_s.at[h - 1], left_r.at[h - 1], right).wait_recv()
+
+            @pl.when(has_left)
+            def _():
+                to_left(h).start()
+
+            to_sibling(nz - 1 + h, me + 2 * h).start()
+
+    to_sibling(0, sib_index).wait_recv()
+    for h in range(1, nz):
+
+        @pl.when(z - h >= 0)
+        def _():
+            to_sibling(h, sib_index - 2 * h).wait_recv()
+
+        @pl.when(z + h < nz)
+        def _():
+            to_sibling(nz - 1 + h, sib_index + 2 * h).wait_recv()
+
+    for t in range(tiles):
+        w_copies[t].wait()
+
+    def exchange(d, t):
+        to = lax.rem(across + d, nn)
+        cols = pl.ds(pl.multiple_of(t * TILE, TILE), TILE)
+        return remote(
+            parts.at[to, :, cols],
+            recv_parts.at[d - 1, :, cols],
+            x_ss.at[d - 1, t],
+            x_rs.at[d - 1, t],
+            {"narrow": to},
+        )
+
+    def multiply(t, carry):
+        acc = jnp.zeros((n_wide * PAD, TILE), jnp.float32)
+        for q in range(PARTS):
+            lhs = held[:, q].reshape(n_wide * PAD, chunk)
+            acc = acc + jnp.dot(
+                lhs,
+                weights[t, pl.ds(q * chunk, chunk), :],
+                preferred_element_type=jnp.float32,
+            )
+        dense = jnp.concatenate(
+            [acc[b * PAD : b * PAD + own_rows] for b in range(n_wide)], axis=0
+        ).astype(jnp.bfloat16)
+        cols = pl.ds(pl.multiple_of(t * TILE, TILE), TILE)
+        for p in range(nn):
+            parts[p, :, cols] = dense[p * out_rows : (p + 1) * out_rows]
+        for d in range(1, nn):
+            exchange(d, t).start()
+        return carry
+
+    lax.fori_loop(0, tiles, multiply, 0)
+
+    def finish(t, carry):
+        cols = pl.ds(pl.multiple_of(t * TILE, TILE), TILE)
+        total = parts[across, :, cols].astype(jnp.float32)
+        for d in range(1, nn):
+            exchange(d, t).wait_recv()
+            total = total + recv_parts[d - 1, :, cols].astype(jnp.float32)
+        out_ref[:, cols] = total.astype(jnp.bfloat16)
+        for d in range(1, nn):
+            exchange(d, t).wait_send()
+        return carry
+
+    lax.fori_loop(0, tiles, finish, 0)
+
+    to_sibling(0, me).wait_send()
+    for h in range(nz):
+
+        @pl.when(jnp.logical_and(z - h >= 0, has_right))
+        def _():
+            to_right(h).wait_send()
+
+        @pl.when(jnp.logical_and(z + h < nz, has_left))
+        def _():
+            to_left(h).wait_send()
+
+        if h > 0:
+
+            @pl.when(z - h >= 0)
+            def _():
+                to_sibling(h, me - 2 * h).wait_send()
+
+            @pl.when(z + h < nz)
+            def _():
+                to_sibling(nz - 1 + h, me + 2 * h).wait_send()
+
+
+def project(heads, w_out, n_wide, nn, own_rows):
+    nz = n_wide // 2
+    depth, cols = w_out.shape
+    chunk = depth // PARTS
+    tiles = cols // TILE
+    out_rows = n_wide * own_rows // nn
+    dma = pltpu.SemaphoreType.DMA
+    return pl.pallas_call(
+        functools.partial(project_kernel, nz, nn, own_rows),
+        out_shape=jax.ShapeDtypeStruct((out_rows, cols), jnp.bfloat16),
+        in_specs=[
+            pl.BlockSpec(memory_space=pltpu.VMEM),
+            pl.BlockSpec(memory_space=pl.ANY),
+        ],
+        out_specs=pl.BlockSpec(memory_space=pltpu.VMEM),
+        scratch_shapes=[
+            pltpu.VMEM((n_wide, PARTS, PAD, chunk), jnp.bfloat16),
+            pltpu.VMEM((tiles, depth, TILE), jnp.bfloat16),
+            pltpu.VMEM((nn, out_rows, cols), jnp.bfloat16),
+            pltpu.VMEM((nn - 1, out_rows, cols), jnp.bfloat16),
+            dma((tiles,)),
+            dma((nz,)),
+            dma((nz,)),
+            dma((nz,)),
+            dma((nz,)),
+            dma((2 * nz - 1,)),
+            dma((2 * nz - 1,)),
+            dma((nn - 1, tiles)),
+            dma((nn - 1, tiles)),
+        ],
+        compiler_params=pltpu.CompilerParams(
+            collective_id=1, has_side_effects=True, vmem_limit_bytes=56 << 20
+        ),
+    )(heads, w_out)
+
+
+def per_device(
+    n_wide, nn, tokens, norm_gain, w_query, w_key, w_value, w_out, cache_key, cache_value, lengths
+):
     all_rows = lax.all_gather(tokens, "narrow", axis=0, tiled=True)
     features = all_rows.astype(jnp.float32)
-    squares = lax.psum_scatter(
-        jnp.sum(features * features, axis=1), "wide", scatter_dimension=0, tiled=True
-    )
-    inverse = lax.rsqrt(squares / D + norm_eps)
+    squares = jnp.sum(features * features, axis=1)
     scaled = (features * norm_gain.astype(jnp.float32)[None, :]).astype(jnp.bfloat16)
     own_rows = cache_key.shape[0]
-    row_start = lax.axis_index("wide") * own_rows
+    index = lax.axis_index("wide")
+    row_start = index * own_rows
     query_cols = w_query.shape[1]
     kv_cols = w_key.shape[1]
-    whole_sums = lax.psum(
-        jnp.concatenate(
-            [
-                jnp.dot(scaled, w_query, preferred_element_type=jnp.float32),
-                jnp.dot(scaled, w_key, preferred_element_type=jnp.float32),
-                jnp.dot(scaled, w_value, preferred_element_type=jnp.float32),
-            ],
-            axis=1,
-        ),
-        "wide",
-    )
-    summed = lax.dynamic_slice_in_dim(whole_sums, row_start, own_rows, 0)
-    summed = summed * inverse[:, None]
+    partial_sums = jnp.concatenate(
+        [
+            jnp.dot(scaled, w_query, preferred_element_type=jnp.float32),
+            jnp.dot(scaled, w_key, preferred_element_type=jnp.float32),
+            jnp.dot(scaled, w_value, preferred_element_type=jnp.float32),
+        ],
+        axis=1,
+    )
+    chip_sums, chip_squares = sum_over_wide(
+        partial_sums, jnp.broadcast_to(squares[:, None], (squares.shape[0], 128)), n_wide
+    )
+    chip_start = lax.rem(index, 2) * own_rows
+    summed = lax.dynamic_slice_in_dim(chip_sums, chip_start, own_rows, 0)
+    mean = lax.dynamic_slice_in_dim(chip_squares, chip_start, own_rows, 0)[:, :1] / D
+    summed = summed * lax.rsqrt(mean + norm_eps)
     own_lengths = lax.dynamic_slice_in_dim(lengths, row_start, own_rows, 0)
     queries = rotate(
         summed[:, :query_cols].reshape(own_rows, query_cols // HD, HD), own_lengths
@@ -101,19 +475,14 @@
         summed[:, query_cols + kv_cols :].reshape(own_rows, kv_cols // HD, HD).astype(jnp.bfloat16)
     )
     heads_out = attend(queries, key_new, value_new, cache_key, cache_value, own_lengths)
-    partials = jnp.dot(
-        lax.all_gather(heads_out, "wide", axis=0, tiled=True),
-        w_out,
-        preferred_element_type=jnp.float32,
-    )
-    return lax.psum_scatter(
-        partials.astype(jnp.bfloat16), "narrow", scatter_dimension=0, tiled=True
-    )
+    stacked = jnp.stack(jnp.split(heads_out, PARTS, axis=1), axis=0)
+    stacked = jnp.pad(stacked, ((0, 0), (0, PAD - own_rows), (0, 0)))
+    return project(stacked, w_out, n_wide, nn, own_rows)
 
 
 def solution(mesh):
     return jax.shard_map(
-        per_device,
+        functools.partial(per_device, mesh.shape["wide"], mesh.shape["narrow"]),
         mesh=mesh,
         in_specs=(
             P(("groups", "narrow"), "wide"),

time: 196 us -> 98.2 us (0.50)
  waiting for transfers between devices: 109 us -> 0 us
  Pallas kernels: 0 us -> 60.3 us
  matrix products: 35.1 us -> 17.9 us
  blocking collectives: 25.3 us -> 8.77 us
  between operations: 13.9 us -> 0.17 us
    psum x1 -> x0, waiting for transfers between devices: 67.2 us -> none  [per_device(): lax.psum(jnp.concatenate([jnp.dot(scaled, w_query, preferred_element_type...]
    pallas_call x0 -> x2, Pallas kernels: none -> 60.3 us  [the longest x1 34.4 us: project(): pl.pallas_call(functools.partial(project_kernel, nz, nn, own_rows), out_s...]
    all_gather x1 -> x0, waiting for transfers between devices: 29.2 us -> none  [per_device(): lax.all_gather(heads_out, 'wide', axis=0, tiled=True)]
    dot_general x1 -> x0, matrix products: 17.3 us -> none  [per_device(): jnp.dot(lax.all_gather(heads_out, 'wide', axis=0, tiled=True), w_out, pre...]
    unnamed x1 -> x0, blocking collectives: 16.4 us -> none
    reduce_scatter x1 -> x0, waiting for transfers between devices: 12.8 us -> none  [per_device(): lax.psum_scatter(partials.astype(jnp.bfloat16), 'narrow', scatter_dimensi...]
    unnamed x16 -> x14, local copies, waits for them, and re-layouts: 5.81 us -> 3.78 us
  transfers between devices with their start and end apart: 3 -> 0, of which waited for: 3 -> 0; matrix products, arithmetic and copies ran while one was open for 1% -> 0% of each run, Pallas kernels for 0% -> 0%
where the time goes in v1:
time: 98.2 us; the launch traced here: 97.8 us
  Pallas kernels  60.3 us (61%)
  matrix products  17.9 us (18%)
  blocking collectives  8.77 us (9%)
  local copies, waits for them, and re-layouts  6.56 us (7%)
  other arithmetic  4.11 us (4%)
    pallas_call x1, Pallas kernels, project(): pl.pallas_call(functools.partial(project_kernel, nz, nn, own_rows), out_s...  34.4 us
    pallas_call x1, Pallas kernels, sum_over_wide(): pl.pallas_call(functools.partial(sums_kernel, nz, steps), out_shape=(jax....  25.9 us
    dot_general x1, matrix products, per_device(): jnp.dot(scaled, w_query, preferred_element_type=jnp.float32)  13.4 us
    all_gather x1, blocking collectives, per_device(): all_rows = lax.all_gather(tokens, 'narrow', axis=0, tiled=True)  8.77 us
    unnamed x14, local copies, waits for them, and re-layouts  3.78 us
    dot_general x1, matrix products, per_device(): jnp.dot(scaled, w_key, preferred_element_type=jnp.float32)  2.08 us

profile of v1, /device:TPU:0, one launch (start us, length us, event | category | flops | bytes accessed | tf_op | source)
XLA Modules:
  0.0 97.8 jit_solution(13186425411597492835)
XLA Ops:
  0.0 0.9 fusion.49
  1.0 0.8 convert_element_type.41
  1.9 8.8 %all_gather.3 = bf16[96,2048]{1,0:T(8,128)(2,1)S(1)} all-gather(bf16[48,2048]{1,0:T(8,128)(2,1)} %param.9), channel_id=1, replica_groups=mesh['groups'=2,'wide'=8,'narrow'=2] {'narrow'}, dimensions={0}, use_global_device_ids=true | all-gather | bytes 589824 | tf_op jit(solution)/shard_map/all_gather | solution.py:442
  10.7 0.2 fusion.19
  11.0 2.1 %fusion.32 = f32[96,512]{1,0:T(8,128)S(1)} fusion(bf16[2048,512]{1,0:T(8,128)(2,1)} %param.12, bf16[96,2048]{1,0:T(8,128)(2,1)S(1)} %all_gather.3, f32[2048]{0:T(1024)S(1)} %convert_element_type.41), kind=kOutput, calls=%fused_computation.31 | convolution fusion | flops 201916416 | bytes 2695168 | tf_op jit(solution)/shard_map/dot_general | solution.py:454
  13.1 0.5 fusion.30
  13.5 13.4 %fusion.34 = f32[96,8192]{1,0:T(8,128)S(1)} fusion(bf16[2048,8192]{1,0:T(8,128)(2,1)} %param.11, bf16[96,2048]{1,0:T(8,128)(2,1)S(1)} %all_gather.3, f32[2048]{0:T(1024)S(1)} %convert_element_type.41), kind=kOutput, calls=%fused_computation.32 | convolution fusion | flops 3221815296 | bytes 37101568 | tf_op jit(solution)/shard_map/dot_general | solution.py:453
  26.9 0.2 pad_maximum_fusion.x_ref
  27.2 25.9 %shard_map.91 = (f32[24,9216]{1,0:T(8,128)S(1)}, f32[24,128]{1,0:T(8,128)S(1)}) custom-call(f32[96,9216]{1,0:T(8,128)S(1)} %pad_maximum_fusion.x_ref, f32[96,128]{1,0:T(8,128)S(1)} %broadcast_in_dim.17.sq_ref), custom_call_target="tpu_custom_call" | custom-call | tf_op jit(solution)/shard_map/pallas_call | solution.py:200
  53.1 0.1 fusion.44
  53.2 0.1 dynamic-slice_multiply_fusion
  53.4 0.8 copy-done.2
  54.2 0.8 slice.36
  54.9 1.9 %slice.33 = f32[12,8192]{1,0:T(8,128)} slice(f32[12,9216]{1,0:T(8,128)} %copy-done.2), slice={[0:12], [0:8192]} | slice | bytes 786432 | tf_op jit(solution)/shard_map/slice | solution.py:468
  56.8 1.1 %copy.18 = f32[2,8,64,128]{3,2,1,0:T(8,128)S(1)} copy(f32[2,8,64,128]{3,1,2,0:T(8,128)} %bitcast.48) | data formatting | bytes 1048576
  58.0 0.2 subtract_convert_fusion
  58.4 0.3 fusion.39
  58.7 1.1 %select_reduce_fusion = (f32[12,4,16]{2,1,0:T(4,128)S(1)}, f32[12,4,16,256]{3,2,1,0:T(8,128)S(1)}) fusion(pred[12,256]{1,0:T(8,128)(4,1)S(1)} %iota_compare_fusion.1, bf16[12,4,16,64]{3,2,1,0:T(8,128)(2,1)S(1)} %bitcast.55, bf16[12,4,16,64]{3,2,1,0:T(8,128)(2,1)S(1)} %bitcast.53, bf16[12,256,512]{2,1,0:T(8,128)(2,1)S(1)} %copy-done), kind=kOutput, calls=%fused_computation.16 | convolution fusion | flops 51313920 | bytes 4134912 | tf_op jit(solution)/shard_map/rgqd,rtgd->rgqt/dot_general | solution.py:49
  59.8 0.4 fusion.20
  60.2 0.6 fusion.15
  60.8 0.2 copy.19
  61.0 0.7 fusion.38.heads_ref
  61.8 34.4 %shard_map.92 = bf16[48,2048]{1,0:T(8,128)(2,1)} custom-call(bf16[4,16,2048]{2,1,0:T(8,128)(2,1)} %fusion.38.heads_ref, bf16[8192,2048]{1,0:T(8,128)(2,1)} %w_ref.1), custom_call_target="tpu_custom_call" | custom-call | tf_op jit(solution)/shard_map/pallas_call | solution.py:410
  96.2 1.6 %copy.41 = bf16[48,2048]{1,0:T(8,128)(2,1)} copy(bf16[48,2048]{1,0:T(8,128)(2,1)} %shard_map.92) | data formatting | bytes 393216
  (23 shorter events, 0.6 us)
Async XLA Ops:
  0.0 58.7 %copy-start = (bf16[12,256,512]{2,1,0:T(8,128)(2,1)S(1)}, bf16[12,256,512]{2,1,0:T(8,128)(2,1)}, u32[]{:S(2)}) copy-start(bf16[12,256,512]{2,1,0:T(8,128)(2,1)} %param.15) | copy-start | bytes 9437188
  0.0 13.0 %copy-start.3 = (bf16[2048,512]{1,0:T(8,128)(2,1)S(1)}, bf16[2048,512]{1,0:T(8,128)(2,1)}, u32[]{:S(2)}) copy-start(bf16[2048,512]{1,0:T(8,128)(2,1)} %param.13) | copy-start | bytes 6291460
  53.3 0.8 copy-start.2
  58.2 2.0 %copy-start.4 = (bf16[12,256,512]{2,1,0:T(8,128)(2,1)S(1)}, bf16[12,256,512]{2,1,0:T(8,128)(2,1)}, u32[]{:S(2)}) copy-start(bf16[12,256,512]{2,1,0:T(8,128)(2,1)} %param.16) | copy-start | bytes 9437188
  61.8 36.0 %copy-start.1 = (bf16[12,256,512]{2,1,0:T(8,128)(2,1)S(1)}, bf16[12,256,512]{2,1,0:T(8,128)(2,1)}, u32[]{:S(2)}) copy-start(bf16[12,256,512]{2,1,0:T(8,128)(2,1)} %param.15) | copy-start | bytes 9437188

commit v2 on v1

--- a/solution.py
+++ b/solution.py
@@ -84,134 +84,200 @@
 
 
 def sums_kernel(
-    nz, steps, x_ref, sq_ref, out_ref, sq_out_ref,
-    core_recv, core_sq, send_buf, recv_buf, sq_send, sq_recv,
-    core_ss, core_rs, csq_s, csq_r, z_ss, z_rs, zsq_ss, zsq_rs, fin_ss, fin_rs,
+    nz, nn, steps, tok_ref, gain_ref, wq_ref, wk_ref, wv_ref, out_ref, sq_out_ref,
+    tok, scaled, sq, weights, x, core_recv, core_sq, send_buf, recv_buf, sq_send, sq_recv,
+    tok_s, tok_r, w_sem, core_ss, core_rs, csq_s, csq_r, z_ss, z_rs, zsq_ss, zsq_rs, fin_ss, fin_rs,
 ):
     me = lax.axis_index("wide")
+    across = lax.axis_index("narrow")
     z, core = me // 2, lax.rem(me, 2)
+    away = 1 - core
     sibling = {"wide": me + 1 - 2 * core}
-    rows, cols = x_ref.shape
+    part_rows = tok_ref.shape[0]
+    rows = part_rows * nn
+    width = wk_ref.shape[1]
     block = rows // nz
-    half = cols // 2
-    width = half // steps
     peers = [lax.rem(z + d, nz) for d in range(1, nz)]
+
+    def query_weights(t, which):
+        start = pl.multiple_of((which * (steps - 1) + t) * width, 128)
+        return pltpu.make_async_copy(
+            wq_ref.at[:, pl.ds(start, width)], weights.at[t, which], w_sem.at[t, which]
+        )
+
+    for t in range(steps - 1):
+        query_weights(t, away).start()
+        query_weights(t, core).start()
+    last = steps - 1
+    pltpu.make_async_copy(wk_ref, weights.at[last, 0], w_sem.at[last, 0]).start()
+    pltpu.make_async_copy(wv_ref, weights.at[last, 1], w_sem.at[last, 1]).start()
+
     barrier = pltpu.get_barrier_semaphore()
-    pl.semaphore_signal(barrier, inc=1, device_id=sibling, device_id_type=MESH)
+
+    def greet(device):
+        pl.semaphore_signal(barrier, inc=1, device_id=device, device_id_type=MESH)
+
+    greet(sibling)
     for peer in peers:
-        pl.semaphore_signal(
-            barrier, inc=1, device_id={"wide": peer * 2 + core}, device_id_type=MESH
-        )
-    pl.semaphore_wait(barrier, nz)
-
-    def columns(which, t):
-        return pl.ds(pl.multiple_of(which * half + t * width, 128), width)
-
-    csq = remote(sq_ref, core_sq, csq_s, csq_r, sibling)
+        greet({"wide": peer * 2 + core})
+    for d in range(1, nn):
+        greet({"narrow": lax.rem(across + d, nn)})
+    pl.semaphore_wait(barrier, nz + nn - 1)
+
+    tok_copies = []
+    for d in range(1, nn):
+        copy = remote(
+            tok_ref,
+            tok.at[d - 1],
+            tok_s.at[d - 1],
+            tok_r.at[d - 1],
+            {"narrow": lax.rem(across + d, nn)},
+        )
+        copy.start()
+        tok_copies.append(copy)
+
+    def take(values, origin):
+        features = values.astype(jnp.float32)
+        span = pl.ds(pl.multiple_of(origin * part_rows, 16), part_rows)
+        total = jnp.sum(features * features, axis=1, keepdims=True)
+        sq[span, :] = jnp.broadcast_to(total, (part_rows, 128))
+        scaled[span, :] = (features * gain_ref[...].astype(jnp.float32)).astype(jnp.bfloat16)
+
+    take(tok_ref[...], across)
+    for d in range(1, nn):
+        tok_copies[d - 1].wait_recv()
+        take(tok[d - 1], lax.rem(across + nn - d, nn))
+
+    csq = remote(sq, core_sq, csq_s, csq_r, sibling)
     csq.start()
-    core_copies = []
-    for t in range(steps):
-        copy = remote(
-            x_ref.at[:, columns(1 - core, t)],
-            core_recv.at[t],
-            core_ss.at[t],
-            core_rs.at[t],
-            sibling,
-        )
-        copy.start()
-        core_copies.append(copy)
-    copies = []
-    csq.wait_recv()
-    for d, peer in enumerate(peers):
-        span = pl.ds(pl.multiple_of(peer * block, 8), block)
-        sq_send[d] = sq_ref[span, :] + core_sq[span, :]
-        copy = remote(
-            sq_send.at[d], sq_recv.at[d], zsq_ss.at[d], zsq_rs.at[d], {"wide": peer * 2 + core}
-        )
-        copy.start()
-        copies.append(copy)
-    z_copies = []
-    for t in range(steps):
-        core_copies[t].wait_recv()
-        row = []
+
+    def to_core(t):
+        return remote(x.at[t, away], core_recv.at[t], core_ss.at[t], core_rs.at[t], sibling)
+
+    def to_chip(t, d):
+        return remote(
+            send_buf.at[t, d],
+            recv_buf.at[t, d],
+            z_ss.at[t, d],
+            z_rs.at[t, d],
+            {"wide": peers[d] * 2 + core},
+        )
+
+    def final(t, which):
+        return remote(
+            out_ref.at[t, which], out_ref.at[t, which], fin_ss.at[t], fin_rs.at[t], sibling
+        )
+
+    def multiply(t, which):
+        pltpu.make_async_copy(
+            wq_ref.at[:, pl.ds(0, width)], weights.at[t, which], w_sem.at[t, which]
+        ).wait()
+        x[t, which] = jnp.dot(
+            scaled[...], weights[t, which], preferred_element_type=jnp.float32
+        )
+
+    def forward(t):
+        to_core(t).wait_recv()
         for d, peer in enumerate(peers):
             span = pl.ds(pl.multiple_of(peer * block, 8), block)
-            both = x_ref[span, columns(core, t)] + core_recv[t, span, :]
+            both = x[t, core, span, :] + core_recv[t, span, :]
             send_buf[t, d] = jnp.concatenate(
                 [both[:, : width // 2], both[:, width // 2 :]], axis=0
             ).astype(jnp.bfloat16)
-            copy = remote(
-                send_buf.at[t, d],
-                recv_buf.at[t, d],
-                z_ss.at[t, d],
-                z_rs.at[t, d],
-                {"wide": peer * 2 + core},
-            )
-            copy.start()
-            row.append(copy)
-        z_copies.append(row)
+            to_chip(t, d).start()
+
+    def step(t, carry):
+        multiply(t, away)
+        to_core(t).start()
+        multiply(t, core)
+
+        @pl.when(t > 0)
+        def _():
+            forward(t - 1)
+
+        return carry
+
+    lax.fori_loop(0, steps, step, 0)
+    forward(steps - 1)
+
+    csq.wait_recv()
+    sq_copies = []
+    for d, peer in enumerate(peers):
+        span = pl.ds(pl.multiple_of(peer * block, 8), block)
+        sq_send[d] = sq[span, :] + core_sq[span, :]
+        copy = remote(
+            sq_send.at[d], sq_recv.at[d], zsq_ss.at[d], zsq_rs.at[d], {"wide": peer * 2 + core}
+        )
+        copy.start()
+        sq_copies.append(copy)
     mine = pl.ds(pl.multiple_of(z * block, 8), block)
-    total = sq_ref[mine, :] + core_sq[mine, :]
-    for d in range(nz - 1):
-        copies[d].wait_recv()
-        total = total + sq_recv[d]
-    sq_out_ref[...] = total
-    finals = []
-    for t in range(steps):
-        acc = x_ref[mine, columns(core, t)] + core_recv[t, mine, :]
+
+    def collect(t, carry):
+        acc = x[t, core, mine, :] + core_recv[t, mine, :]
         left, right = acc[:, : width // 2], acc[:, width // 2 :]
         for d in range(nz - 1):
-            z_copies[t][d].wait_recv()
+            to_chip(t, d).wait_recv()
             got = recv_buf[t, d].astype(jnp.float32)
             left = left + got[:block]
             right = right + got[block:]
-        out_ref[:, columns(core, t)] = jnp.concatenate([left, right], axis=1)
-        copy = remote(
-            out_ref.at[:, columns(core, t)],
-            out_ref.at[:, columns(core, t)],
-            fin_ss.at[t],
-            fin_rs.at[t],
-            sibling,
-        )
-        copy.start()
-        finals.append(copy)
+        out_ref[t, core] = jnp.concatenate([left, right], axis=1)
+        final(t, core).start()
+        return carry
+
+    lax.fori_loop(0, steps, collect, 0)
+    total = sq[mine, :] + core_sq[mine, :]
+    for d in range(nz - 1):
+        sq_copies[d].wait_recv()
+        total = total + sq_recv[d]
+    sq_out_ref[...] = total
+
+    def drain(t, carry):
+        to_core(t).wait_send()
+        for d in range(nz - 1):
+            to_chip(t, d).wait_send()
+        final(t, core).wait_send()
+        final(t, away).wait_recv()
+        return carry
+
+    lax.fori_loop(0, steps, drain, 0)
     csq.wait_send()
-    for copy in core_copies + copies + sum(z_copies, []):
+    for copy in tok_copies + sq_copies:
         copy.wait_send()
-    for t in range(steps):
-        finals[t].wait_send()
-        remote(
-            out_ref.at[:, columns(1 - core, t)],
-            out_ref.at[:, columns(1 - core, t)],
-            fin_ss.at[t],
-            fin_rs.at[t],
-            sibling,
-        ).wait_recv()
-
-
-def sum_over_wide(x, sq, n_wide):
+
+
+def project_in(tokens, norm_gain, w_query, w_key, w_value, n_wide, nn):
     nz = n_wide // 2
-    rows, cols = x.shape
+    part_rows, depth = tokens.shape
+    rows = part_rows * nn
     block = rows // nz
-    steps = 3
-    width = cols // 2 // steps
+    width = w_key.shape[1]
+    steps = w_query.shape[1] // (2 * width) + 1
     vmem = pl.BlockSpec(memory_space=pltpu.VMEM)
+    hbm = pl.BlockSpec(memory_space=pl.ANY)
     dma = pltpu.SemaphoreType.DMA
     return pl.pallas_call(
-        functools.partial(sums_kernel, nz, steps),
+        functools.partial(sums_kernel, nz, nn, steps),
         out_shape=(
-            jax.ShapeDtypeStruct((block, cols), jnp.float32),
+            jax.ShapeDtypeStruct((steps, 2, block, width), jnp.float32),
             jax.ShapeDtypeStruct((block, 128), jnp.float32),
         ),
-        in_specs=[vmem, vmem],
+        in_specs=[vmem, vmem, hbm, hbm, hbm],
         out_specs=(vmem, vmem),
         scratch_shapes=[
+            pltpu.VMEM((nn - 1, part_rows, depth), jnp.bfloat16),
+            pltpu.VMEM((rows, depth), jnp.bfloat16),
+            pltpu.VMEM((rows, 128), jnp.float32),
+            pltpu.VMEM((steps, 2, depth, width), jnp.bfloat16),
+            pltpu.VMEM((steps, 2, rows, width), jnp.float32),
             pltpu.VMEM((steps, rows, width), jnp.float32),
             pltpu.VMEM((rows, 128), jnp.float32),
             pltpu.VMEM((steps, nz - 1, 2 * block, width // 2), jnp.bfloat16),
             pltpu.VMEM((steps, nz - 1, 2 * block, width // 2), jnp.bfloat16),
             pltpu.VMEM((nz - 1, block, 128), jnp.float32),
             pltpu.VMEM((nz - 1, block, 128), jnp.float32),
+            dma((nn - 1,)),
+            dma((nn - 1,)),
+            dma((steps, 2)),
             dma((steps,)),
             dma((steps,)),
             dma,
@@ -224,9 +290,9 @@
             dma((steps,)),
         ],
         compiler_params=pltpu.CompilerParams(
-            collective_id=0, has_side_effects=True, vmem_limit_bytes=48 << 20
+            collective_id=0, has_side_effects=True, vmem_limit_bytes=56 << 20
         ),
-    )(x, sq)
+    )(tokens, norm_gain[None, :], w_query, w_key, w_value)
 
 
 def project_kernel(
@@ -439,29 +505,25 @@
 def per_device(
     n_wide, nn, tokens, norm_gain, w_query, w_key, w_value, w_out, cache_key, cache_value, lengths
 ):
-    all_rows = lax.all_gather(tokens, "narrow", axis=0, tiled=True)
-    features = all_rows.astype(jnp.float32)
-    squares = jnp.sum(features * features, axis=1)
-    scaled = (features * norm_gain.astype(jnp.float32)[None, :]).astype(jnp.bfloat16)
     own_rows = cache_key.shape[0]
     index = lax.axis_index("wide")
     row_start = index * own_rows
     query_cols = w_query.shape[1]
     kv_cols = w_key.shape[1]
-    partial_sums = jnp.concatenate(
+    chip_sums, chip_squares = project_in(
+        tokens, norm_gain, w_query, w_key, w_value, n_wide, nn
+    )
+    chip_start = lax.rem(index, 2) * own_rows
+    mean = lax.dynamic_slice_in_dim(chip_squares, chip_start, own_rows, 0)[:, :1] / D
+    own_sums = lax.dynamic_slice_in_dim(chip_sums, chip_start, own_rows, 2)
+    last = own_sums.shape[0] - 1
+    summed = jnp.concatenate(
         [
-            jnp.dot(scaled, w_query, preferred_element_type=jnp.float32),
-            jnp.dot(scaled, w_key, preferred_element_type=jnp.float32),
-            jnp.dot(scaled, w_value, preferred_element_type=jnp.float32),
+            own_sums[:last].transpose(2, 1, 0, 3).reshape(own_rows, query_cols),
+            own_sums[last].transpose(1, 0, 2).reshape(own_rows, 2 * kv_cols),
         ],
         axis=1,
     )
-    chip_sums, chip_squares = sum_over_wide(
-        partial_sums, jnp.broadcast_to(squares[:, None], (squares.shape[0], 128)), n_wide
-    )
-    chip_start = lax.rem(index, 2) * own_rows
-    summed = lax.dynamic_slice_in_dim(chip_sums, chip_start, own_rows, 0)
-    mean = lax.dynamic_slice_in_dim(chip_squares, chip_start, own_rows, 0)[:, :1] / D
     summed = summed * lax.rsqrt(mean + norm_eps)
     own_lengths = lax.dynamic_slice_in_dim(lengths, row_start, own_rows, 0)
     queries = rotate(

time: 98.2 us -> 88.1 us (0.90)
  matrix products: 17.9 us -> 1.97 us
  Pallas kernels: 60.3 us -> 71.4 us
  blocking collectives: 8.77 us -> 0 us
  local copies, waits for them, and re-layouts: 6.56 us -> 10.6 us
    dot_general x3 -> x0, matrix products: 15.9 us -> none  [the longest x1 13.4 us: per_device(): jnp.dot(scaled, w_query, preferred_element_type=jnp.float32)]
    pallas_call x1, Pallas kernels: 25.9 us -> 37.9 us  [project_in(): pl.pallas_call(functools.partial(sums_kernel, nz, nn, steps), out_shape=(...]
    all_gather x1 -> x0, blocking collectives: 8.77 us -> none  [per_device(): all_rows = lax.all_gather(tokens, 'narrow', axis=0, tiled=True)]
    transpose x0 -> x4, local copies, waits for them, and re-layouts: none -> 2.4 us  [the longest x2 1.45 us: per_device(): own_sums[:last].transpose(2, 1, 0, 3).reshape(own_rows, query_cols)]
    broadcast_in_dim x1, local copies, waits for them, and re-layouts: 0.08 us -> 1.29 us  [project_in(): norm_gain[None, :]]
    unnamed x14 -> x16, local copies, waits for them, and re-layouts: 3.78 us -> 4.18 us
where the time goes in v2:
time: 88.1 us; the launch traced here: 87.6 us
  Pallas kernels  71.4 us (81%)
  local copies, waits for them, and re-layouts  10.6 us (12%)
  other arithmetic  3.54 us (4%)
  matrix products  1.97 us (2%)
    pallas_call x1, Pallas kernels, project_in(): pl.pallas_call(functools.partial(sums_kernel, nz, nn, steps), out_shape=(...  37.9 us
    pallas_call x1, Pallas kernels, project(): pl.pallas_call(functools.partial(project_kernel, nz, nn, own_rows), out_s...  33.5 us
    unnamed x16, local copies, waits for them, and re-layouts  4.18 us
    slice x1, local copies, waits for them, and re-layouts, per_device(): summed[:, :query_cols].reshape(own_rows, query_cols // HD, HD)  1.87 us

profile of v2, /device:TPU:0, one launch (start us, length us, event | category | flops | bytes accessed | tf_op | source)
XLA Modules:
  0.0 87.6 jit_solution(1068138313426778090)
XLA Ops:
  0.0 0.9 %fusion.41 = (f32[12]{0:T(128)S(1)}, s32[12]{0:T(128)S(1)}) fusion(s32[96]{0:T(128)} %param.17, s32[]{:T(128)S(6)} %select_n.14), kind=kLoop, calls=%fused_computation.57 | loop fusion | flops 12 | bytes 148 | tf_op jit(solution)/shard_map/convert_element_type | solution.py:25
  1.0 1.3 %broadcast_in_dim.21.gain_ref = bf16[1,2048]{1,0:T(2,128)(2,1)} reshape(bf16[2048]{0:T(1024)(128)(2,1)} %param.10) | data formatting | bytes 8192 | tf_op jit(solution)/shard_map/broadcast_in_dim | solution.py:295
  2.3 0.1 multiply_cosine_fusion
  2.4 37.9 %shard_map.91 = (f32[9,2,24,512]{3,2,1,0:T(8,128)}, f32[24,128]{1,0:T(8,128)}) custom-call(bf16[48,2048]{1,0:T(8,128)(2,1)} %tok_ref.1, bf16[1,2048]{1,0:T(2,128)(2,1)} %broadcast_in_dim.21.gain_ref, bf16[2048,8192]{1,0:T(8,128)(2,1)} %wq_ref.1, bf16[2048,512]{1,0:T(8,128)(2,1)} %wk_ref.1, bf16[2048,512]{1,0:T(8,128)(2,1)} %wv_ref.1), custom_call_target="tpu_custom_call" | custom-call | tf_op jit(solution)/shard_map/pallas_call | solution.py:258
  40.3 0.8 fusion.36
  41.1 0.9 %dynamic-slice_bitcast_fusion.1 = f32[12,2,512]{2,0,1:T(8,128)S(1)} fusion(f32[9,2,24,512]{3,2,1,0:T(8,128)} %get-tuple-element.7, s32[]{:T(128)S(6)} %add.32, s32[]{:T(128)S(6)} %select_n.15), kind=kLoop, calls=%fused_computation.35 | loop fusion | bytes 98312 | tf_op jit(solution)/shard_map/transpose | solution.py:523
  42.0 1.2 %dynamic-slice_bitcast_fusion = f32[12,2,8,512]{3,0,1,2:T(8,128)S(1)} fusion(f32[9,2,24,512]{3,2,1,0:T(8,128)} %get-tuple-element.7, s32[]{:T(128)S(6)} %select_n.15), kind=kLoop, calls=%fused_computation.20 | loop fusion | bytes 786436 | tf_op jit(solution)/shard_map/transpose | solution.py:522
  43.2 0.2 copy.45
  43.6 0.3 copy.20
  43.9 0.1 maximum_multiply_fusion
  44.1 0.8 copy-done.2
  44.9 0.8 slice.44
  45.7 1.9 %slice.41 = f32[12,8192]{1,0:T(8,128)} slice(f32[12,9216]{1,0:T(8,128)} %copy-done.2), slice={[0:12], [0:8192]} | slice | bytes 786432 | tf_op jit(solution)/shard_map/slice | solution.py:530
  47.5 1.1 %copy.22 = f32[2,8,64,128]{3,2,1,0:T(8,128)S(1)} copy(f32[2,8,64,128]{3,1,2,0:T(8,128)} %bitcast.61) | data formatting | bytes 1048576
  48.7 0.2 subtract_convert_fusion
  48.9 0.1 subtract_convert_fusion.1
  49.1 0.3 fusion.31
  49.4 1.1 %select_reduce_fusion = (f32[12,4,16]{2,1,0:T(4,128)S(1)}, f32[12,4,16,256]{3,2,1,0:T(8,128)S(1)}) fusion(pred[12,256]{1,0:T(8,128)(4,1)S(1)} %iota_compare_fusion.1, bf16[12,4,16,64]{3,2,1,0:T(8,128)(2,1)S(1)} %bitcast.70, bf16[12,4,16,64]{3,2,1,0:T(8,128)(2,1)S(1)} %bitcast.68, bf16[12,256,512]{2,1,0:T(8,128)(2,1)S(1)} %copy-done), kind=kOutput, calls=%fused_computation.11 | convolution fusion | flops 51313920 | bytes 4134912 | tf_op jit(solution)/shard_map/rgqd,rtgd->rgqt/dot_general | solution.py:49
  50.5 0.4 fusion.18
  50.9 0.6 fusion.15
  51.5 0.2 copy.23
  51.8 0.7 fusion.30.heads_ref
  52.5 33.5 %shard_map.92 = bf16[48,2048]{1,0:T(8,128)(2,1)} custom-call(bf16[4,16,2048]{2,1,0:T(8,128)(2,1)} %fusion.30.heads_ref, bf16[8192,2048]{1,0:T(8,128)(2,1)} %w_ref.1), custom_call_target="tpu_custom_call" | custom-call | tf_op jit(solution)/shard_map/pallas_call | solution.py:476
  86.0 1.6 %copy.47 = bf16[48,2048]{1,0:T(8,128)(2,1)} copy(bf16[48,2048]{1,0:T(8,128)(2,1)} %shard_map.92) | data formatting | bytes 393216
  (22 shorter events, 0.5 us)
Async XLA Ops:
  0.0 49.4 %copy-start = (bf16[12,256,512]{2,1,0:T(8,128)(2,1)S(1)}, bf16[12,256,512]{2,1,0:T(8,128)(2,1)}, u32[]{:S(2)}) copy-start(bf16[12,256,512]{2,1,0:T(8,128)(2,1)} %param.15) | copy-start | bytes 9437188
  44.1 0.8 copy-start.2
  48.9 2.0 %copy-start.3 = (bf16[12,256,512]{2,1,0:T(8,128)(2,1)S(1)}, bf16[12,256,512]{2,1,0:T(8,128)(2,1)}, u32[]{:S(2)}) copy-start(bf16[12,256,512]{2,1,0:T(8,128)(2,1)} %param.16) | copy-start | bytes 9437188
  52.5 35.1 %copy-start.1 = (bf16[12,256,512]{2,1,0:T(8,128)(2,1)S(1)}, bf16[12,256,512]{2,1,0:T(8,128)(2,1)}, u32[]{:S(2)}) copy-start(bf16[12,256,512]{2,1,0:T(8,128)(2,1)} %param.15) | copy-start | bytes 9437188

commit v3 on v2

--- a/solution.py
+++ b/solution.py
@@ -9,8 +9,8 @@
 
 D = 16384
 HD = 128
-PAD = 16
 PARTS = 4
+CHUNKS = 4
 TILE = 256
 MESH = pl.DeviceIdType.MESH
 
@@ -297,7 +297,7 @@
 
 def project_kernel(
     nz, nn, own_rows, heads_ref, w_ref, out_ref,
-    held, weights, parts, recv_parts,
+    held, lhs, weights, total_ref, parts, recv_parts,
     w_sem, right_s, left_s, right_r, left_r, sib_s, sib_r, x_ss, x_rs,
 ):
     me = lax.axis_index("wide")
@@ -309,15 +309,16 @@
     has_right, has_left = z < nz - 1, z > 0
     n_wide = 2 * nz
     tiles = w_ref.shape[1] // TILE
-    chunk = w_ref.shape[0] // PARTS
+    piece = w_ref.shape[0] // (PARTS * CHUNKS)
     out_rows = out_ref.shape[0]
 
-    w_copies = []
-    for t in range(tiles):
-        cols = pl.ds(t * TILE, TILE)
-        copy = pltpu.make_async_copy(w_ref.at[:, cols], weights.at[t], w_sem.at[t])
-        copy.start()
-        w_copies.append(copy)
+    def fetch(s, q):
+        span = pl.ds((q * CHUNKS + s) * piece, piece)
+        return pltpu.make_async_copy(w_ref.at[span, :], weights.at[s, q], w_sem.at[s, q])
+
+    for s in range(CHUNKS):
+        for q in range(PARTS):
+            fetch(s, q).start()
 
     barrier = pltpu.get_barrier_semaphore()
 
@@ -339,65 +340,72 @@
     ends = jnp.where(has_right, 1, 0) + jnp.where(has_left, 1, 0)
     pl.semaphore_wait(barrier, nn + ends)
 
-    def to_right(h):
-        slot = held.at[me - 2 * h]
-        return remote(slot, slot, right_s.at[h], right_r.at[h], right)
-
-    def to_left(h):
-        slot = held.at[me + 2 * h]
-        return remote(slot, slot, left_s.at[h], left_r.at[h], left)
-
-    def to_sibling(k, index):
-        return remote(held.at[index], held.at[index], sib_s.at[k], sib_r.at[k], sibling)
+    def to_right(h, s):
+        slot = held.at[me - 2 * h, s]
+        return remote(slot, slot, right_s.at[h, s], right_r.at[h, s], right)
+
+    def to_left(h, s):
+        slot = held.at[me + 2 * h, s]
+        return remote(slot, slot, left_s.at[h, s], left_r.at[h, s], left)
+
+    def to_sibling(k, s, index):
+        slot = held.at[index, s]
+        return remote(slot, slot, sib_s.at[k, s], sib_r.at[k, s], sibling)
 
     held[me] = heads_ref[...]
 
-    @pl.when(has_right)
-    def _():
-        to_right(0).start()
-
-    @pl.when(has_left)
-    def _():
-        to_left(0).start()
-
-    to_sibling(0, me).start()
-    for h in range(1, nz):
-
+    def send_own(s):
+        @pl.when(has_right)
+        def _():
+            to_right(0, s).start()
+
+        @pl.when(has_left)
+        def _():
+            to_left(0, s).start()
+
+        to_sibling(0, s, me).start()
+
+    def relay(h, s):
         @pl.when(z - h >= 0)
         def _():
-            slot = held.at[me - 2 * h]
-            remote(slot, slot, right_s.at[h - 1], right_r.at[h - 1], left).wait_recv()
+            slot = held.at[me - 2 * h, s]
+            remote(slot, slot, right_s.at[h - 1, s], right_r.at[h - 1, s], left).wait_recv()
 
             @pl.when(has_right)
             def _():
-                to_right(h).start()
-
-            to_sibling(h, me - 2 * h).start()
+                to_right(h, s).start()
+
+            to_sibling(h, s, me - 2 * h).start()
 
         @pl.when(z + h < nz)
         def _():
-            slot = held.at[me + 2 * h]
-            remote(slot, slot, left_s.at[h - 1], left_r.at[h - 1], right).wait_recv()
+            slot = held.at[me + 2 * h, s]
+            remote(slot, slot, left_s.at[h - 1, s], left_r.at[h - 1, s], right).wait_recv()
 
             @pl.when(has_left)
             def _():
-                to_left(h).start()
-
-            to_sibling(nz - 1 + h, me + 2 * h).start()
-
-    to_sibling(0, sib_index).wait_recv()
-    for h in range(1, nz):
-
-        @pl.when(z - h >= 0)
-        def _():
-            to_sibling(h, sib_index - 2 * h).wait_recv()
-
-        @pl.when(z + h < nz)
-        def _():
-            to_sibling(nz - 1 + h, sib_index + 2 * h).wait_recv()
-
-    for t in range(tiles):
-        w_copies[t].wait()
+                to_left(h, s).start()
+
+            to_sibling(nz - 1 + h, s, me + 2 * h).start()
+
+    def from_sibling(s):
+        to_sibling(0, s, sib_index).wait_recv()
+        for h in range(1, nz):
+
+            @pl.when(z - h >= 0)
+            def _():
+                to_sibling(h, s, sib_index - 2 * h).wait_recv()
+
+            @pl.when(z + h < nz)
+            def _():
+                to_sibling(nz - 1 + h, s, sib_index + 2 * h).wait_recv()
+
+    def gather_rows(s):
+        blocks = [held[b, s].astype(jnp.float32) for b in range(n_wide)]
+        for q in range(PARTS):
+            rows = [block[q * own_rows : (q + 1) * own_rows] for block in blocks]
+            lhs[q] = jnp.concatenate(rows, axis=0).astype(jnp.bfloat16)
+            fetch(s, q).wait()
 
     def exchange(d, t):
         to = lax.rem(across + d, nn)
@@ -410,18 +418,40 @@
             {"narrow": to},
         )
 
-    def multiply(t, carry):
-        acc = jnp.zeros((n_wide * PAD, TILE), jnp.float32)
+    def product(s, t):
+        cols = pl.ds(pl.multiple_of(t * TILE, TILE), TILE)
+        acc = None if s == 0 else total_ref[:, cols]
         for q in range(PARTS):
-            lhs = held[:, q].reshape(n_wide * PAD, chunk)
-            acc = acc + jnp.dot(
-                lhs,
-                weights[t, pl.ds(q * chunk, chunk), :],
-                preferred_element_type=jnp.float32,
-            )
-        dense = jnp.concatenate(
-            [acc[b * PAD : b * PAD + own_rows] for b in range(n_wide)], axis=0
-        ).astype(jnp.bfloat16)
+            term = jnp.dot(lhs[q], weights[s, q, :, cols], preferred_element_type=jnp.float32)
+            acc = term if acc is None else acc + term
+        return acc
+
+    def multiply(s, first, end):
+        def body(t, carry):
+            cols = pl.ds(pl.multiple_of(t * TILE, TILE), TILE)
+            total_ref[:, cols] = product(s, t)
+            return carry
+
+        lax.fori_loop(first, end, body, 0)
+
+    send_own(0)
+    for h in range(1, nz):
+        if h == 1:
+            send_own(1)
+        relay(h, 0)
+    from_sibling(0)
+    for s in range(CHUNKS - 1):
+        gather_rows(s)
+        if s + 2 < CHUNKS:
+            send_own(s + 2)
+        for h in range(1, nz):
+            relay(h, s + 1)
+            multiply(s, (h - 1) * tiles // (nz - 1), h * tiles // (nz - 1))
+        from_sibling(s + 1)
+    gather_rows(CHUNKS - 1)
+
+    def last_multiply(t, carry):
+        dense = product(CHUNKS - 1, t).astype(jnp.bfloat16)
         cols = pl.ds(pl.multiple_of(t * TILE, TILE), TILE)
         for p in range(nn):
             parts[p, :, cols] = dense[p * out_rows : (p + 1) * out_rows]
@@ -429,7 +459,7 @@
             exchange(d, t).start()
         return carry
 
-    lax.fori_loop(0, tiles, multiply, 0)
+    lax.fori_loop(0, tiles, last_multiply, 0)
 
     def finish(t, carry):
         cols = pl.ds(pl.multiple_of(t * TILE, TILE), TILE)
@@ -444,32 +474,33 @@
 
     lax.fori_loop(0, tiles, finish, 0)
 
-    to_sibling(0, me).wait_send()
-    for h in range(nz):
-
-        @pl.when(jnp.logical_and(z - h >= 0, has_right))
-        def _():
-            to_right(h).wait_send()
-
-        @pl.when(jnp.logical_and(z + h < nz, has_left))
-        def _():
-            to_left(h).wait_send()
-
-        if h > 0:
-
-            @pl.when(z - h >= 0)
+    for s in range(CHUNKS):
+        to_sibling(0, s, me).wait_send()
+        for h in range(nz):
+
+            @pl.when(jnp.logical_and(z - h >= 0, has_right))
             def _():
-                to_sibling(h, me - 2 * h).wait_send()
-
-            @pl.when(z + h < nz)
+                to_right(h, s).wait_send()
+
+            @pl.when(jnp.logical_and(z + h < nz, has_left))
             def _():
-                to_sibling(nz - 1 + h, me + 2 * h).wait_send()
+                to_left(h, s).wait_send()
+
+            if h > 0:
+
+                @pl.when(z - h >= 0)
+                def _():
+                    to_sibling(h, s, me - 2 * h).wait_send()
+
+                @pl.when(z + h < nz)
+                def _():
+                    to_sibling(nz - 1 + h, s, me + 2 * h).wait_send()
 
 
 def project(heads, w_out, n_wide, nn, own_rows):
     nz = n_wide // 2
     depth, cols = w_out.shape
-    chunk = depth // PARTS
+    piece = depth // (PARTS * CHUNKS)
     tiles = cols // TILE
     out_rows = n_wide * own_rows // nn
     dma = pltpu.SemaphoreType.DMA
@@ -482,17 +513,19 @@
         ],
         out_specs=pl.BlockSpec(memory_space=pltpu.VMEM),
         scratch_shapes=[
-            pltpu.VMEM((n_wide, PARTS, PAD, chunk), jnp.bfloat16),
-            pltpu.VMEM((tiles, depth, TILE), jnp.bfloat16),
+            pltpu.VMEM((n_wide, CHUNKS, PARTS * own_rows, piece), jnp.bfloat16),
+            pltpu.VMEM((PARTS, n_wide * own_rows, piece), jnp.bfloat16),
+            pltpu.VMEM((CHUNKS, PARTS, piece, cols), jnp.bfloat16),
+            pltpu.VMEM((n_wide * own_rows, cols), jnp.float32),
             pltpu.VMEM((nn, out_rows, cols), jnp.bfloat16),
             pltpu.VMEM((nn - 1, out_rows, cols), jnp.bfloat16),
-            dma((tiles,)),
-            dma((nz,)),
-            dma((nz,)),
-            dma((nz,)),
-            dma((nz,)),
-            dma((2 * nz - 1,)),
-            dma((2 * nz - 1,)),
+            dma((CHUNKS, PARTS)),
+            dma((nz, CHUNKS)),
+            dma((nz, CHUNKS)),
+            dma((nz, CHUNKS)),
+            dma((nz, CHUNKS)),
+            dma((2 * nz - 1, CHUNKS)),
+            dma((2 * nz - 1, CHUNKS)),
             dma((nn - 1, tiles)),
             dma((nn - 1, tiles)),
         ],
@@ -537,8 +570,9 @@
         summed[:, query_cols + kv_cols :].reshape(own_rows, kv_cols // HD, HD).astype(jnp.bfloat16)
     )
     heads_out = attend(queries, key_new, value_new, cache_key, cache_value, own_lengths)
-    stacked = jnp.stack(jnp.split(heads_out, PARTS, axis=1), axis=0)
-    stacked = jnp.pad(stacked, ((0, 0), (0, PAD - own_rows), (0, 0)))
+    piece = query_cols // (PARTS * CHUNKS)
+    stacked = heads_out.reshape(own_rows, PARTS, CHUNKS, piece).transpose(2, 1, 0, 3)
+    stacked = stacked.reshape(CHUNKS, PARTS * own_rows, piece)
     return project(stacked, w_out, n_wide, nn, own_rows)
 
 

time: 88.1 us -> 91.8 us (1.042)
  Pallas kernels: 71.4 us -> 75.2 us
    pallas_call x1, Pallas kernels: 33.5 us -> 37.4 us  [project(): pl.pallas_call(functools.partial(project_kernel, nz, nn, own_rows), out_s...]
    unnamed x16 -> x14, local copies, waits for them, and re-layouts: 4.18 us -> 3.97 us
where the time goes in v3:
time: 91.8 us; the launch traced here: 91.4 us
  Pallas kernels  75.2 us (82%)
  local copies, waits for them, and re-layouts  11.2 us (12%)
  other arithmetic  2.79 us (3%)
  matrix products  1.97 us (2%)
    pallas_call x1, Pallas kernels, project_in(): pl.pallas_call(functools.partial(sums_kernel, nz, nn, steps), out_shape=(...  37.9 us
    pallas_call x1, Pallas kernels, project(): pl.pallas_call(functools.partial(project_kernel, nz, nn, own_rows), out_s...  37.4 us
    unnamed x14, local copies, waits for them, and re-layouts  3.97 us
    slice x1, local copies, waits for them, and re-layouts, per_device(): summed[:, :query_cols].reshape(own_rows, query_cols // HD, HD)  1.87 us

profile of v3, /device:TPU:0, one launch (start us, length us, event | category | flops | bytes accessed | tf_op | source)
XLA Modules:
  0.0 91.4 jit_solution(7557911245810162404)
XLA Ops:
  0.0 0.9 fusion.34
  1.0 1.3 %broadcast_in_dim.21.gain_ref = bf16[1,2048]{1,0:T(2,128)(2,1)} reshape(bf16[2048]{0:T(1024)(128)(2,1)} %param.10) | data formatting | bytes 8192 | tf_op jit(solution)/shard_map/broadcast_in_dim | solution.py:295
  2.3 0.1 multiply_cosine_fusion
  2.4 37.9 %shard_map.91 = (f32[9,2,24,512]{3,2,1,0:T(8,128)}, f32[24,128]{1,0:T(8,128)}) custom-call(bf16[48,2048]{1,0:T(8,128)(2,1)} %tok_ref.1, bf16[1,2048]{1,0:T(2,128)(2,1)} %broadcast_in_dim.21.gain_ref, bf16[2048,8192]{1,0:T(8,128)(2,1)} %wq_ref.1, bf16[2048,512]{1,0:T(8,128)(2,1)} %wk_ref.1, bf16[2048,512]{1,0:T(8,128)(2,1)} %wv_ref.1), custom_call_target="tpu_custom_call" | custom-call | tf_op jit(solution)/shard_map/pallas_call | solution.py:258
  40.3 0.8 fusion.29
  41.1 0.9 dynamic-slice_bitcast_fusion.1
  42.0 1.2 %dynamic-slice_bitcast_fusion = f32[12,2,8,512]{3,0,1,2:T(8,128)S(1)} fusion(f32[9,2,24,512]{3,2,1,0:T(8,128)} %get-tuple-element.7, s32[]{:T(128)S(6)} %select_n.15), kind=kLoop, calls=%fused_computation.15 | loop fusion | bytes 786436 | tf_op jit(solution)/shard_map/transpose | solution.py:555
  43.2 0.2 copy.47
  43.6 0.3 copy.23
  43.9 0.1 maximum_multiply_fusion
  44.1 0.8 copy-done.2
  44.9 0.8 slice.44
  45.6 1.9 %slice.41 = f32[12,8192]{1,0:T(8,128)} slice(f32[12,9216]{1,0:T(8,128)} %copy-done.2), slice={[0:12], [0:8192]} | slice | bytes 786432 | tf_op jit(solution)/shard_map/slice | solution.py:563
  47.5 1.1 %copy.25 = f32[2,8,64,128]{3,2,1,0:T(8,128)S(1)} copy(f32[2,8,64,128]{3,1,2,0:T(8,128)} %bitcast.54) | data formatting | bytes 1048576
  48.7 0.2 subtract_convert_fusion
  48.9 0.1 subtract_convert_fusion.1
  49.1 0.3 fusion.24
  49.4 1.1 %select_reduce_fusion = (f32[12,4,16]{2,1,0:T(4,128)S(1)}, f32[12,4,16,256]{3,2,1,0:T(8,128)S(1)}) fusion(pred[12,256]{1,0:T(8,128)(4,1)S(1)} %iota_compare_fusion, bf16[12,4,16,64]{3,2,1,0:T(8,128)(2,1)S(1)} %bitcast.61, bf16[12,4,16,64]{3,2,1,0:T(8,128)(2,1)S(1)} %bitcast.59, bf16[12,256,512]{2,1,0:T(8,128)(2,1)S(1)} %copy-done), kind=kOutput, calls=%fused_computation.11 | convolution fusion | flops 51313920 | bytes 4134912 | tf_op jit(solution)/shard_map/rgqd,rtgd->rgqt/dot_general | solution.py:49
  50.5 0.4 fusion.18
  50.9 0.6 fusion.15
  51.5 0.1 reshape_reshape.3
  51.7 0.7 copy.18.heads_ref
  52.4 37.4 %shard_map.92 = bf16[48,2048]{1,0:T(8,128)(2,1)} custom-call(bf16[4,48,512]{2,1,0:T(8,128)(2,1)} %copy.18.heads_ref, bf16[8192,2048]{1,0:T(8,128)(2,1)} %w_ref.1), custom_call_target="tpu_custom_call" | custom-call | tf_op jit(solution)/shard_map/pallas_call | solution.py:507
  89.8 1.6 %copy.49 = bf16[48,2048]{1,0:T(8,128)(2,1)} copy(bf16[48,2048]{1,0:T(8,128)(2,1)} %shard_map.92) | data formatting | bytes 393216
  (21 shorter events, 0.5 us)
Async XLA Ops:
  0.0 49.4 %copy-start = (bf16[12,256,512]{2,1,0:T(8,128)(2,1)S(1)}, bf16[12,256,512]{2,1,0:T(8,128)(2,1)}, u32[]{:S(2)}) copy-start(bf16[12,256,512]{2,1,0:T(8,128)(2,1)} %param.15) | copy-start | bytes 9437188
  44.1 0.8 copy-start.2
  48.9 2.0 %copy-start.3 = (bf16[12,256,512]{2,1,0:T(8,128)(2,1)S(1)}, bf16[12,256,512]{2,1,0:T(8,128)(2,1)}, u32[]{:S(2)}) copy-start(bf16[12,256,512]{2,1,0:T(8,128)(2,1)} %param.16) | copy-start | bytes 9437188
  52.4 39.0 %copy-start.1 = (bf16[12,256,512]{2,1,0:T(8,128)(2,1)S(1)}, bf16[12,256,512]{2,1,0:T(8,128)(2,1)}, u32[]{:S(2)}) copy-start(bf16[12,256,512]{2,1,0:T(8,128)(2,1)} %param.15) | copy-start | bytes 9437188

commit v4 on v3

--- a/solution.py
+++ b/solution.py
@@ -10,8 +10,8 @@
 D = 16384
 HD = 128
 PARTS = 4
-CHUNKS = 4
-TILE = 256
+CHUNKS = 2
+TILE = 512
 MESH = pl.DeviceIdType.MESH
 
 
@@ -141,7 +141,7 @@
         span = pl.ds(pl.multiple_of(origin * part_rows, 16), part_rows)
         total = jnp.sum(features * features, axis=1, keepdims=True)
         sq[span, :] = jnp.broadcast_to(total, (part_rows, 128))
-        scaled[span, :] = (features * gain_ref[...].astype(jnp.float32)).astype(jnp.bfloat16)
+        scaled[span, :] = (features * gain_ref[...]).astype(jnp.bfloat16)
 
     take(tok_ref[...], across)
     for d in range(1, nn):
@@ -292,7 +292,7 @@
         compiler_params=pltpu.CompilerParams(
             collective_id=0, has_side_effects=True, vmem_limit_bytes=56 << 20
         ),
-    )(tokens, norm_gain[None, :], w_query, w_key, w_value)
+    )(tokens, norm_gain.astype(jnp.float32)[None, :], w_query, w_key, w_value)
 
 
 def project_kernel(
@@ -436,9 +436,9 @@
 
     send_own(0)
     for h in range(1, nz):
+        relay(h, 0)
         if h == 1:
             send_own(1)
-        relay(h, 0)
     from_sibling(0)
     for s in range(CHUNKS - 1):
         gather_rows(s)
@@ -550,25 +550,14 @@
     mean = lax.dynamic_slice_in_dim(chip_squares, chip_start, own_rows, 0)[:, :1] / D
     own_sums = lax.dynamic_slice_in_dim(chip_sums, chip_start, own_rows, 2)
     last = own_sums.shape[0] - 1
-    summed = jnp.concatenate(
-        [
-            own_sums[:last].transpose(2, 1, 0, 3).reshape(own_rows, query_cols),
-            own_sums[last].transpose(1, 0, 2).reshape(own_rows, 2 * kv_cols),
-        ],
-        axis=1,
-    )
-    summed = summed * lax.rsqrt(mean + norm_eps)
+    inverse = lax.rsqrt(mean + norm_eps)[:, :, None]
+    own_queries = own_sums[:last].transpose(2, 1, 0, 3).reshape(own_rows, query_cols // HD, HD)
+    own_key = own_sums[last, 0].reshape(own_rows, kv_cols // HD, HD)
+    own_value = own_sums[last, 1].reshape(own_rows, kv_cols // HD, HD)
     own_lengths = lax.dynamic_slice_in_dim(lengths, row_start, own_rows, 0)
-    queries = rotate(
-        summed[:, :query_cols].reshape(own_rows, query_cols // HD, HD), own_lengths
-    ).astype(jnp.bfloat16)
-    key_new = rotate(
-        summed[:, query_cols : query_cols + kv_cols].reshape(own_rows, kv_cols // HD, HD),
-        own_lengths,
-    ).astype(jnp.bfloat16)
-    value_new = (
-        summed[:, query_cols + kv_cols :].reshape(own_rows, kv_cols // HD, HD).astype(jnp.bfloat16)
-    )
+    queries = rotate(own_queries * inverse, own_lengths).astype(jnp.bfloat16)
+    key_new = rotate(own_key * inverse, own_lengths).astype(jnp.bfloat16)
+    value_new = (own_value * inverse).astype(jnp.bfloat16)
     heads_out = attend(queries, key_new, value_new, cache_key, cache_value, own_lengths)
     piece = query_cols // (PARTS * CHUNKS)
     stacked = heads_out.reshape(own_rows, PARTS, CHUNKS, piece).transpose(2, 1, 0, 3)

time: 91.8 us -> 83.4 us (0.908)
  Pallas kernels: 75.2 us -> 67.6 us
  local copies, waits for them, and re-layouts: 11.2 us -> 5.65 us
  other arithmetic: 2.79 us -> 6.79 us
    pallas_call x1, Pallas kernels: 37.4 us -> 29.7 us  [project(): pl.pallas_call(functools.partial(project_kernel, nz, nn, own_rows), out_s...]
    unnamed x14 -> x13, local copies, waits for them, and re-layouts: 3.97 us -> 1.64 us
    slice x2 -> x1, local copies, waits for them, and re-layouts: 2.63 us -> 0.84 us  [per_device(): own_value = own_sums[last, 1].reshape(own_rows, kv_cols // HD, HD)]
    broadcast_in_dim x0 -> x1, other arithmetic: none -> 1.44 us  [project_in(): norm_gain.astype(jnp.float32)[None, :]]
    broadcast_in_dim x1 -> x0, local copies, waits for them, and re-layouts: 1.29 us -> none  [project_in(): norm_gain[None, :]]
    mul x1, other arithmetic: 0.11 us -> 1.09 us  [per_device(): queries = rotate(own_queries * inverse, own_lengths).astype(jnp.bfloat16)]
    transpose x4 -> x2, local copies, waits for them, and re-layouts: 2.4 us -> 1.44 us  [per_device(): own_sums[:last].transpose(2, 1, 0, 3)]
where the time goes in v4:
time: 83.4 us; the launch traced here: 83.1 us
  Pallas kernels  67.6 us (81%)
  other arithmetic  6.79 us (8%)
  local copies, waits for them, and re-layouts  5.65 us (7%)
  matrix products  2.87 us (3%)
    pallas_call x1, Pallas kernels, project_in(): pl.pallas_call(functools.partial(sums_kernel, nz, nn, steps), out_shape=(...  37.9 us
    pallas_call x1, Pallas kernels, project(): pl.pallas_call(functools.partial(project_kernel, nz, nn, own_rows), out_s...  29.7 us

profile of v4, /device:TPU:0, one launch (start us, length us, event | category | flops | bytes accessed | tf_op | source)
XLA Modules:
  0.0 83.1 jit_solution(8315738235144774531)
XLA Ops:
  0.0 1.4 %broadcast_in_dim.44 = f32[2048]{0:T(1024)} convert(bf16[2048]{0:T(1024)(128)(2,1)} %param.10) | non-fusion elementwise | flops 2048 | bytes 12288 | tf_op jit(solution)/shard_map/broadcast_in_dim | solution.py:295
  1.4 37.9 %shard_map.91 = (f32[9,2,24,512]{3,2,1,0:T(8,128)}, f32[24,128]{1,0:T(8,128)}) custom-call(bf16[48,2048]{1,0:T(8,128)(2,1)} %tok_ref.1, f32[1,2048]{1,0:T(1,128)} %bitcast.47, bf16[2048,8192]{1,0:T(8,128)(2,1)} %wq_ref.1, bf16[2048,512]{1,0:T(8,128)(2,1)} %wk_ref.1, bf16[2048,512]{1,0:T(8,128)(2,1)} %wv_ref.1), custom_call_target="tpu_custom_call" | custom-call | tf_op jit(solution)/shard_map/pallas_call | solution.py:258
  39.3 0.8 %constant_dynamic-slice_fusion.1 = (f32[1,1,12,512]{3,2,1,0:T(8,128)S(1)}, f32[1,1,12,512]{3,2,1,0:T(8,128)S(1)}) fusion(f32[9,2,24,512]{3,2,1,0:T(8,128)} %get-tuple-element.7, s32[]{:T(128)S(6)} %add.30, s32[]{:T(128)S(6)} %add.32, s32[]{:T(128)S(6)} %select_n.15), kind=kLoop, calls=%fused_computation.40 | loop fusion | bytes 98316 | tf_op jit(solution)/shard_map/slice | solution.py:556
  40.2 0.8 %fusion.29 = f32[12]{0:T(128)S(1)} fusion(f32[24,128]{1,0:T(8,128)} %get-tuple-element.8, s32[]{:T(128)S(6)} %select_n.15), kind=kLoop, calls=%fused_computation.38 | loop fusion | flops 24 | bytes 100 | tf_op jit(solution)/shard_map/rsqrt | solution.py:553
  41.0 0.7 fusion.26
  41.7 0.6 fusion.34
  42.3 0.1 multiply_cosine_fusion
  42.5 0.1 subtract_convert_fusion.1
  42.6 0.7 maximum_bitcast_fusion
  43.2 1.2 %dynamic-slice_bitcast_fusion = f32[12,2,8,512]{3,0,1,2:T(8,128)S(1)} fusion(f32[9,2,24,512]{3,2,1,0:T(8,128)} %get-tuple-element.7, s32[]{:T(128)S(6)} %select_n.15), kind=kLoop, calls=%fused_computation.14 | loop fusion | bytes 786436 | tf_op jit(solution)/shard_map/transpose | solution.py:554
  44.4 0.2 copy.13
  44.7 0.8 reshape.96
  45.5 1.1 %broadcast_multiply_fusion = f32[12,64,128]{2,1,0:T(8,128)S(1)} fusion(f32[12,64,128]{2,1,0:T(8,128)} %reshape.96, f32[12]{0:T(128)} %copy-done.3), kind=kLoop, calls=%fused_computation.21 | loop fusion | flops 98304 | bytes 786480 | tf_op jit(solution)/shard_map/mul | solution.py:558
  46.6 0.2 subtract_convert_fusion
  46.8 1.1 %fusion.24 = f32[12,4,1,16]{3,2,1,0:T(1,128)S(1)} fusion(bf16[12,4,16,64]{3,2,1,0:T(8,128)(2,1)S(1)} %bitcast.42, bf16[12,4,16,64]{3,2,1,0:T(8,128)(2,1)S(1)} %bitcast.40, bf16[12,4,128,1]{2,1,0,3:T(4,128)(2,1)} %maximum_bitcast_fusion), kind=kOutput, calls=%fused_computation.22 | convolution fusion | flops 589824 | bytes 211968 | tf_op jit(solution)/shard_map/rgqd,rgd->rgq/dot_general | solution.py:53
  47.9 0.7 iota_compare_fusion
  48.6 1.1 %select_reduce_fusion = (f32[12,4,16]{2,1,0:T(4,128)S(1)}, f32[12,4,16,256]{3,2,1,0:T(8,128)S(1)}) fusion(pred[12,256]{1,0:T(8,128)(4,1)S(1)} %iota_compare_fusion, bf16[12,4,16,64]{3,2,1,0:T(8,128)(2,1)S(1)} %bitcast.43, bf16[12,4,16,64]{3,2,1,0:T(8,128)(2,1)S(1)} %bitcast.41, bf16[12,256,512]{2,1,0:T(8,128)(2,1)S(1)} %copy-done), kind=kOutput, calls=%fused_computation.11 | convolution fusion | flops 51313920 | bytes 4134912 | tf_op jit(solution)/shard_map/rgqd,rtgd->rgqt/dot_general | solution.py:49
  49.7 0.4 fusion.18
  50.1 0.7 fusion.15
  50.8 0.1 reshape_reshape.3
  50.9 0.1 copy.16
  51.0 0.7 copy.17.heads_ref
  51.7 29.7 %shard_map.92 = bf16[48,2048]{1,0:T(8,128)(2,1)} custom-call(bf16[2,48,1024]{2,1,0:T(8,128)(2,1)} %copy.17.heads_ref, bf16[8192,2048]{1,0:T(8,128)(2,1)} %w_ref.1), custom_call_target="tpu_custom_call" | custom-call | tf_op jit(solution)/shard_map/pallas_call | solution.py:507
  81.4 1.6 %copy.43 = bf16[48,2048]{1,0:T(8,128)(2,1)} copy(bf16[48,2048]{1,0:T(8,128)(2,1)} %shard_map.92) | data formatting | bytes 393216
  (17 shorter events, 0.1 us)
Async XLA Ops:
  0.0 48.6 %copy-start = (bf16[12,256,512]{2,1,0:T(8,128)(2,1)S(1)}, bf16[12,256,512]{2,1,0:T(8,128)(2,1)}, u32[]{:S(2)}) copy-start(bf16[12,256,512]{2,1,0:T(8,128)(2,1)} %param.15) | copy-start | bytes 9437188
  1.4 40.3 %copy-start.4 = (s32[96]{0:T(128)S(1)}, s32[96]{0:T(128)}, u32[]{:S(2)}) copy-start(s32[96]{0:T(128)} %param.17) | copy-start | bytes 1156
  41.0 1.4 %copy-start.3 = (f32[12]{0:T(128)}, f32[12]{0:T(128)S(1)}, u32[]{:S(2)}) copy-start(f32[12]{0:T(128)S(1)} %fusion.29) | copy-start | bytes 148
  46.8 3.3 %copy-start.2 = (f32[12,4,128]{2,1,0:T(4,128)S(1)}, f32[12,4,128]{2,1,0:T(4,128)}, u32[]{:S(2)}) copy-start(f32[12,4,128]{2,1,0:T(4,128)} %get-tuple-element.21) | copy-start | bytes 73732
  46.8 3.3 %copy-start.5 = (bf16[12,256,512]{2,1,0:T(8,128)(2,1)S(1)}, bf16[12,256,512]{2,1,0:T(8,128)(2,1)}, u32[]{:S(2)}) copy-start(bf16[12,256,512]{2,1,0:T(8,128)(2,1)} %param.16) | copy-start | bytes 9437188
  51.7 31.3 %copy-start.1 = (bf16[12,256,512]{2,1,0:T(8,128)(2,1)S(1)}, bf16[12,256,512]{2,1,0:T(8,128)(2,1)}, u32[]{:S(2)}) copy-start(bf16[12,256,512]{2,1,0:T(8,128)(2,1)} %param.15) | copy-start | bytes 9437188

commit v5 on v4

--- a/solution.py
+++ b/solution.py
@@ -105,12 +105,16 @@
             wq_ref.at[:, pl.ds(start, width)], weights.at[t, which], w_sem.at[t, which]
         )
 
-    for t in range(steps - 1):
+    last = steps - 1
+    ahead = min(3, last)
+
+    def fetch_kv():
+        pltpu.make_async_copy(wk_ref, weights.at[last, 0], w_sem.at[last, 0]).start()
+        pltpu.make_async_copy(wv_ref, weights.at[last, 1], w_sem.at[last, 1]).start()
+
+    for t in range(ahead):
         query_weights(t, away).start()
         query_weights(t, core).start()
-    last = steps - 1
-    pltpu.make_async_copy(wk_ref, weights.at[last, 0], w_sem.at[last, 0]).start()
-    pltpu.make_async_copy(wv_ref, weights.at[last, 1], w_sem.at[last, 1]).start()
 
     barrier = pltpu.get_barrier_semaphore()
 
@@ -141,7 +145,7 @@
         span = pl.ds(pl.multiple_of(origin * part_rows, 16), part_rows)
         total = jnp.sum(features * features, axis=1, keepdims=True)
         sq[span, :] = jnp.broadcast_to(total, (part_rows, 128))
-        scaled[span, :] = (features * gain_ref[...]).astype(jnp.bfloat16)
+        scaled[span, :] = (features * gain_ref[...][None, :]).astype(jnp.bfloat16)
 
     take(tok_ref[...], across)
     for d in range(1, nn):
@@ -187,6 +191,15 @@
             to_chip(t, d).start()
 
     def step(t, carry):
+        @pl.when(t + ahead < last)
+        def _():
+            query_weights(t + ahead, away).start()
+            query_weights(t + ahead, core).start()
+
+        @pl.when(t + ahead == last)
+        def _():
+            fetch_kv()
+
         multiply(t, away)
         to_core(t).start()
         multiply(t, core)
@@ -292,7 +305,7 @@
         compiler_params=pltpu.CompilerParams(
             collective_id=0, has_side_effects=True, vmem_limit_bytes=56 << 20
         ),
-    )(tokens, norm_gain.astype(jnp.float32)[None, :], w_query, w_key, w_value)
+    )(tokens, norm_gain.astype(jnp.float32), w_query, w_key, w_value)
 
 
 def project_kernel(
@@ -316,9 +329,8 @@
         span = pl.ds((q * CHUNKS + s) * piece, piece)
         return pltpu.make_async_copy(w_ref.at[span, :], weights.at[s, q], w_sem.at[s, q])
 
-    for s in range(CHUNKS):
-        for q in range(PARTS):
-            fetch(s, q).start()
+    for q in range(PARTS):
+        fetch(0, q).start()
 
     barrier = pltpu.get_barrier_semaphore()
 
@@ -442,6 +454,8 @@
     from_sibling(0)
     for s in range(CHUNKS - 1):
         gather_rows(s)
+        for q in range(PARTS):
+            fetch(s + 1, q).start()
         if s + 2 < CHUNKS:
             send_own(s + 2)
         for h in range(1, nz):

time: 83.4 us -> 83.9 us (level)
    broadcast_in_dim x1 -> x0, other arithmetic: 1.44 us -> none  [project_in(): norm_gain.astype(jnp.float32)[None, :]]
    convert_element_type x0 -> x1, other arithmetic: none -> 1.44 us  [project_in(): norm_gain.astype(jnp.float32)]
where the time goes in v5:
time: 83.9 us; the launch traced here: 83.6 us
  Pallas kernels  68.1 us (81%)
  other arithmetic  6.79 us (8%)
  local copies, waits for them, and re-layouts  5.65 us (7%)
  matrix products  2.87 us (3%)
    pallas_call x1, Pallas kernels, project_in(): pl.pallas_call(functools.partial(sums_kernel, nz, nn, steps), out_shape=(...  37.9 us
    pallas_call x1, Pallas kernels, project(): pl.pallas_call(functools.partial(project_kernel, nz, nn, own_rows), out_s...  30.2 us

profile of v5, /device:TPU:0, one launch (start us, length us, event | category | flops | bytes accessed | tf_op | source)
XLA Modules:
  0.0 83.6 jit_solution(7720469923822339190)
XLA Ops:
  0.0 1.4 %convert_element_type.30.gain_ref = f32[2048]{0:T(1024)} convert(bf16[2048]{0:T(1024)(128)(2,1)} %param.10) | non-fusion elementwise | flops 2048 | bytes 12288 | tf_op jit(solution)/shard_map/convert_element_type | solution.py:308
  1.4 37.9 %shard_map.91 = (f32[9,2,24,512]{3,2,1,0:T(8,128)}, f32[24,128]{1,0:T(8,128)}) custom-call(bf16[48,2048]{1,0:T(8,128)(2,1)} %tok_ref.1, f32[2048]{0:T(1024)} %convert_element_type.30.gain_ref, bf16[2048,8192]{1,0:T(8,128)(2,1)} %wq_ref.1, bf16[2048,512]{1,0:T(8,128)(2,1)} %wk_ref.1, bf16[2048,512]{1,0:T(8,128)(2,1)} %wv_ref.1), custom_call_target="tpu_custom_call" | custom-call | tf_op jit(solution)/shard_map/pallas_call | solution.py:271
  39.3 0.8 %constant_dynamic-slice_fusion.1 = (f32[1,1,12,512]{3,2,1,0:T(8,128)S(1)}, f32[1,1,12,512]{3,2,1,0:T(8,128)S(1)}) fusion(f32[9,2,24,512]{3,2,1,0:T(8,128)} %get-tuple-element.7, s32[]{:T(128)S(6)} %add.30, s32[]{:T(128)S(6)} %add.32, s32[]{:T(128)S(6)} %select_n.15), kind=kLoop, calls=%fused_computation.40 | loop fusion | bytes 98316 | tf_op jit(solution)/shard_map/slice | solution.py:570
  40.2 0.8 fusion.29
  41.0 0.7 fusion.26
  41.7 0.6 fusion.34
  42.3 0.1 multiply_cosine_fusion
  42.5 0.1 subtract_convert_fusion.1
  42.6 0.7 maximum_bitcast_fusion
  43.2 1.2 %dynamic-slice_bitcast_fusion = f32[12,2,8,512]{3,0,1,2:T(8,128)S(1)} fusion(f32[9,2,24,512]{3,2,1,0:T(8,128)} %get-tuple-element.7, s32[]{:T(128)S(6)} %select_n.15), kind=kLoop, calls=%fused_computation.14 | loop fusion | bytes 786436 | tf_op jit(solution)/shard_map/transpose | solution.py:568
  44.4 0.2 copy.13
  44.7 0.8 reshape.96
  45.5 1.1 %broadcast_multiply_fusion = f32[12,64,128]{2,1,0:T(8,128)S(1)} fusion(f32[12,64,128]{2,1,0:T(8,128)} %reshape.96, f32[12]{0:T(128)} %copy-done.3), kind=kLoop, calls=%fused_computation.21 | loop fusion | flops 98304 | bytes 786480 | tf_op jit(solution)/shard_map/mul | solution.py:572
  46.6 0.2 subtract_convert_fusion
  46.8 1.1 %fusion.24 = f32[12,4,1,16]{3,2,1,0:T(1,128)S(1)} fusion(bf16[12,4,16,64]{3,2,1,0:T(8,128)(2,1)S(1)} %bitcast.41, bf16[12,4,16,64]{3,2,1,0:T(8,128)(2,1)S(1)} %bitcast.39, bf16[12,4,128,1]{2,1,0,3:T(4,128)(2,1)} %maximum_bitcast_fusion), kind=kOutput, calls=%fused_computation.22 | convolution fusion | flops 589824 | bytes 211968 | tf_op jit(solution)/shard_map/rgqd,rgd->rgq/dot_general | solution.py:53
  47.9 0.7 iota_compare_fusion
  48.6 1.1 %select_reduce_fusion = (f32[12,4,16]{2,1,0:T(4,128)S(1)}, f32[12,4,16,256]{3,2,1,0:T(8,128)S(1)}) fusion(pred[12,256]{1,0:T(8,128)(4,1)S(1)} %iota_compare_fusion, bf16[12,4,16,64]{3,2,1,0:T(8,128)(2,1)S(1)} %bitcast.42, bf16[12,4,16,64]{3,2,1,0:T(8,128)(2,1)S(1)} %bitcast.40, bf16[12,256,512]{2,1,0:T(8,128)(2,1)S(1)} %copy-done), kind=kOutput, calls=%fused_computation.11 | convolution fusion | flops 51313920 | bytes 4134912 | tf_op jit(solution)/shard_map/rgqd,rtgd->rgqt/dot_general | solution.py:49
  49.7 0.4 fusion.18
  50.1 0.7 fusion.15
  50.8 0.1 reshape_reshape.3
  50.9 0.1 copy.16
  51.0 0.7 copy.17.heads_ref
  51.7 30.2 %shard_map.92 = bf16[48,2048]{1,0:T(8,128)(2,1)} custom-call(bf16[2,48,1024]{2,1,0:T(8,128)(2,1)} %copy.17.heads_ref, bf16[8192,2048]{1,0:T(8,128)(2,1)} %w_ref.1), custom_call_target="tpu_custom_call" | custom-call | tf_op jit(solution)/shard_map/pallas_call | solution.py:521
  81.9 1.6 %copy.43 = bf16[48,2048]{1,0:T(8,128)(2,1)} copy(bf16[48,2048]{1,0:T(8,128)(2,1)} %shard_map.92) | data formatting | bytes 393216
  (17 shorter events, 0.1 us)
Async XLA Ops:
  0.0 48.6 %copy-start = (bf16[12,256,512]{2,1,0:T(8,128)(2,1)S(1)}, bf16[12,256,512]{2,1,0:T(8,128)(2,1)}, u32[]{:S(2)}) copy-start(bf16[12,256,512]{2,1,0:T(8,128)(2,1)} %param.15) | copy-start | bytes 9437188
  1.4 40.3 %copy-start.4 = (s32[96]{0:T(128)S(1)}, s32[96]{0:T(128)}, u32[]{:S(2)}) copy-start(s32[96]{0:T(128)} %param.17) | copy-start | bytes 1156
  41.0 1.4 %copy-start.3 = (f32[12]{0:T(128)}, f32[12]{0:T(128)S(1)}, u32[]{:S(2)}) copy-start(f32[12]{0:T(128)S(1)} %fusion.29) | copy-start | bytes 148
  46.8 3.3 %copy-start.2 = (f32[12,4,128]{2,1,0:T(4,128)S(1)}, f32[12,4,128]{2,1,0:T(4,128)}, u32[]{:S(2)}) copy-start(f32[12,4,128]{2,1,0:T(4,128)} %get-tuple-element.21) | copy-start | bytes 73732
  46.8 3.3 %copy-start.5 = (bf16[12,256,512]{2,1,0:T(8,128)(2,1)S(1)}, bf16[12,256,512]{2,1,0:T(8,128)(2,1)}, u32[]{:S(2)}) copy-start(bf16[12,256,512]{2,1,0:T(8,128)(2,1)} %param.16) | copy-start | bytes 9437188
  51.7 31.8 %copy-start.1 = (bf16[12,256,512]{2,1,0:T(8,128)(2,1)S(1)}, bf16[12,256,512]{2,1,0:T(8,128)(2,1)}, u32[]{:S(2)}) copy-start(bf16[12,256,512]{2,1,0:T(8,128)(2,1)} %param.15) | copy-start | bytes 9437188

commit v6 on v4

--- a/solution.py
+++ b/solution.py
@@ -141,7 +141,7 @@
         span = pl.ds(pl.multiple_of(origin * part_rows, 16), part_rows)
         total = jnp.sum(features * features, axis=1, keepdims=True)
         sq[span, :] = jnp.broadcast_to(total, (part_rows, 128))
-        scaled[span, :] = (features * gain_ref[...]).astype(jnp.bfloat16)
+        scaled[span, :] = (features * gain_ref[...].astype(jnp.float32)[None, :]).astype(jnp.bfloat16)
 
     take(tok_ref[...], across)
     for d in range(1, nn):
@@ -292,7 +292,7 @@
         compiler_params=pltpu.CompilerParams(
             collective_id=0, has_side_effects=True, vmem_limit_bytes=56 << 20
         ),
-    )(tokens, norm_gain.astype(jnp.float32)[None, :], w_query, w_key, w_value)
+    )(tokens, norm_gain, w_query, w_key, w_value)
 
 
 def project_kernel(

time: 83.4 us -> 82.1 us (0.984)
  other arithmetic: 6.79 us -> 5.36 us
    broadcast_in_dim x1 -> x0, other arithmetic: 1.44 us -> none  [project_in(): norm_gain.astype(jnp.float32)[None, :]]
where the time goes in v6:
time: 82.1 us; the launch traced here: 81.8 us
  Pallas kernels  67.7 us (82%)
  local copies, waits for them, and re-layouts  5.65 us (7%)
  other arithmetic  5.36 us (7%)
  matrix products  2.87 us (3%)
    pallas_call x1, Pallas kernels, project_in(): pl.pallas_call(functools.partial(sums_kernel, nz, nn, steps), out_shape=(...  38 us
    pallas_call x1, Pallas kernels, project(): pl.pallas_call(functools.partial(project_kernel, nz, nn, own_rows), out_s...  29.7 us
    unnamed x13, local copies, waits for them, and re-layouts  1.64 us

profile of v6, /device:TPU:0, one launch (start us, length us, event | category | flops | bytes accessed | tf_op | source)
XLA Modules:
  0.0 81.8 jit_solution(10488969153483933540)
XLA Ops:
  0.0 38.0 %shard_map.91 = (f32[9,2,24,512]{3,2,1,0:T(8,128)}, f32[24,128]{1,0:T(8,128)}) custom-call(bf16[48,2048]{1,0:T(8,128)(2,1)} %tok_ref.1, bf16[2048]{0:T(1024)(128)(2,1)} %gain_ref.1, bf16[2048,8192]{1,0:T(8,128)(2,1)} %wq_ref.1, bf16[2048,512]{1,0:T(8,128)(2,1)} %wk_ref.1, bf16[2048,512]{1,0:T(8,128)(2,1)} %wv_ref.1), custom_call_target="tpu_custom_call" | custom-call | tf_op jit(solution)/shard_map/pallas_call | solution.py:258
  38.0 0.8 %constant_dynamic-slice_fusion.1 = (f32[1,1,12,512]{3,2,1,0:T(8,128)S(1)}, f32[1,1,12,512]{3,2,1,0:T(8,128)S(1)}) fusion(f32[9,2,24,512]{3,2,1,0:T(8,128)} %get-tuple-element.7, s32[]{:T(128)S(6)} %add.30, s32[]{:T(128)S(6)} %add.32, s32[]{:T(128)S(6)} %select_n.15), kind=kLoop, calls=%fused_computation.40 | loop fusion | bytes 98316 | tf_op jit(solution)/shard_map/slice | solution.py:556
  38.9 0.8 %fusion.29 = f32[12]{0:T(128)S(1)} fusion(f32[24,128]{1,0:T(8,128)} %get-tuple-element.8, s32[]{:T(128)S(6)} %select_n.15), kind=kLoop, calls=%fused_computation.38 | loop fusion | flops 24 | bytes 100 | tf_op jit(solution)/shard_map/rsqrt | solution.py:553
  39.8 0.7 fusion.26
  40.5 0.6 fusion.34
  41.1 0.1 multiply_cosine_fusion
  41.2 0.1 subtract_convert_fusion.1
  41.3 0.7 maximum_bitcast_fusion
  42.0 1.2 %dynamic-slice_bitcast_fusion = f32[12,2,8,512]{3,0,1,2:T(8,128)S(1)} fusion(f32[9,2,24,512]{3,2,1,0:T(8,128)} %get-tuple-element.7, s32[]{:T(128)S(6)} %select_n.15), kind=kLoop, calls=%fused_computation.14 | loop fusion | bytes 786436 | tf_op jit(solution)/shard_map/transpose | solution.py:554
  43.2 0.2 copy.13
  43.4 0.8 reshape.96
  44.2 1.1 %broadcast_multiply_fusion = f32[12,64,128]{2,1,0:T(8,128)S(1)} fusion(f32[12,64,128]{2,1,0:T(8,128)} %reshape.96, f32[12]{0:T(128)} %copy-done.3), kind=kLoop, calls=%fused_computation.21 | loop fusion | flops 98304 | bytes 786480 | tf_op jit(solution)/shard_map/mul | solution.py:558
  45.3 0.2 subtract_convert_fusion
  45.5 0.0 copy-start.2
  45.5 1.1 %fusion.24 = f32[12,4,1,16]{3,2,1,0:T(1,128)S(1)} fusion(bf16[12,4,16,64]{3,2,1,0:T(8,128)(2,1)S(1)} %bitcast.41, bf16[12,4,16,64]{3,2,1,0:T(8,128)(2,1)S(1)} %bitcast.39, bf16[12,4,128,1]{2,1,0,3:T(4,128)(2,1)} %maximum_bitcast_fusion), kind=kOutput, calls=%fused_computation.22 | convolution fusion | flops 589824 | bytes 211968 | tf_op jit(solution)/shard_map/rgqd,rgd->rgq/dot_general | solution.py:53
  46.7 0.7 iota_compare_fusion
  47.3 1.1 %select_reduce_fusion = (f32[12,4,16]{2,1,0:T(4,128)S(1)}, f32[12,4,16,256]{3,2,1,0:T(8,128)S(1)}) fusion(pred[12,256]{1,0:T(8,128)(4,1)S(1)} %iota_compare_fusion, bf16[12,4,16,64]{3,2,1,0:T(8,128)(2,1)S(1)} %bitcast.42, bf16[12,4,16,64]{3,2,1,0:T(8,128)(2,1)S(1)} %bitcast.40, bf16[12,256,512]{2,1,0:T(8,128)(2,1)S(1)} %copy-done), kind=kOutput, calls=%fused_computation.11 | convolution fusion | flops 51313920 | bytes 4134912 | tf_op jit(solution)/shard_map/rgqd,rtgd->rgqt/dot_general | solution.py:49
  48.4 0.4 fusion.18
  48.8 0.7 fusion.15
  49.5 0.1 reshape_reshape.3
  49.6 0.1 copy.16
  49.7 0.7 copy.17.heads_ref
  50.4 29.7 %shard_map.92 = bf16[48,2048]{1,0:T(8,128)(2,1)} custom-call(bf16[2,48,1024]{2,1,0:T(8,128)(2,1)} %copy.17.heads_ref, bf16[8192,2048]{1,0:T(8,128)(2,1)} %w_ref.1), custom_call_target="tpu_custom_call" | custom-call | tf_op jit(solution)/shard_map/pallas_call | solution.py:507
  80.2 1.6 %copy.43 = bf16[48,2048]{1,0:T(8,128)(2,1)} copy(bf16[48,2048]{1,0:T(8,128)(2,1)} %shard_map.92) | data formatting | bytes 393216
  (16 shorter events, 0.1 us)
Async XLA Ops:
  0.0 47.3 %copy-start = (bf16[12,256,512]{2,1,0:T(8,128)(2,1)S(1)}, bf16[12,256,512]{2,1,0:T(8,128)(2,1)}, u32[]{:S(2)}) copy-start(bf16[12,256,512]{2,1,0:T(8,128)(2,1)} %param.15) | copy-start | bytes 9437188
  0.0 40.5 %copy-start.4 = (s32[96]{0:T(128)S(1)}, s32[96]{0:T(128)}, u32[]{:S(2)}) copy-start(s32[96]{0:T(128)} %param.17) | copy-start | bytes 1156
  39.8 1.4 %copy-start.3 = (f32[12]{0:T(128)}, f32[12]{0:T(128)S(1)}, u32[]{:S(2)}) copy-start(f32[12]{0:T(128)S(1)} %fusion.29) | copy-start | bytes 148
  45.5 3.3 %copy-start.2 = (f32[12,4,128]{2,1,0:T(4,128)S(1)}, f32[12,4,128]{2,1,0:T(4,128)}, u32[]{:S(2)}) copy-start(f32[12,4,128]{2,1,0:T(4,128)} %get-tuple-element.21) | copy-start | bytes 73732
  45.5 3.3 %copy-start.5 = (bf16[12,256,512]{2,1,0:T(8,128)(2,1)S(1)}, bf16[12,256,512]{2,1,0:T(8,128)(2,1)}, u32[]{:S(2)}) copy-start(bf16[12,256,512]{2,1,0:T(8,128)(2,1)} %param.16) | copy-start | bytes 9437188
  50.4 31.3 %copy-start.1 = (bf16[12,256,512]{2,1,0:T(8,128)(2,1)S(1)}, bf16[12,256,512]{2,1,0:T(8,128)(2,1)}, u32[]{:S(2)}) copy-start(bf16[12,256,512]{2,1,0:T(8,128)(2,1)} %param.15) | copy-start | bytes 9437188
